TPU v7x, 32 devices: a whole 2x2x4 slice. The times are simulated.
32 devices in a mesh: set: 1, kb: 32 (over z, y, x, core).
Axes of the slice: x: 2, y: 2, z: 4, core: 2. Of those that a mesh axis runs over, the one named last changes fastest.
Arguments:
- green_momentum_grid: float32 [2, 4, 4096, 512], P('set', None, 'kb'), may hold values from -6 to 6
- pair_table: int32 [8, 2], replicated, may hold values from 0 to 3, as said below
- mirror_map: int32 [3, 16], P('set'), may hold values from 0 to 15, as said below
Outputs:
- chi_out: float32 [2, 8, 4096, 512], P('set', None, 'kb')
Inputs may be any that keep to these rules, and one draw needn't show every extreme that they name: `pair_table`: each of the two columns names every entry number 0 to 3 at least once. Each row d is a reflection: mirror_map[d,x] = (c_d - x) mod 16 for a centre c_d of that row.
All inputs are finite; a program needn't handle non-finite values.
Results may differ from a plain program's by a relative error of at most 0.0003.
Values sent between devices are 32-bit elements; how exact they have to be, the bound alone decides.
No kernel may reach another device: no remote copies, remote signals or barrier semaphores. Data moves between devices by JAX's collectives and lax.ppermute only.
A program may use at most 128 MiB of HBM per device.

v0:
```python
import functools

import jax
import jax.numpy as jnp
import ml_dtypes
import numpy as np
from jax import lax
from jax.experimental import pallas as pl
from jax.experimental.pallas import tpu as pltpu
from jax.sharding import PartitionSpec as P

LANES = 128
ROWS = 8
GROUPS = 1


def split_constant(matrix):
    high = matrix.astype(np.float32).astype(ml_dtypes.bfloat16)
    low = (matrix - high.astype(np.float64)).astype(np.float32).astype(ml_dtypes.bfloat16)
    return high, low


def split_value(value):
    high = value.astype(jnp.bfloat16)
    low = (value - high.astype(jnp.float32)).astype(jnp.bfloat16)
    return high, low


def dot3(left, right, dims):
    def one(a, b):
        return lax.dot_general(a, b, (dims, ((), ())), preferred_element_type=jnp.float32)

    return one(left[0], right[0]) + (one(left[0], right[1]) + one(left[1], right[0]))


def time_rows(devices, pairs, padded):
    rows = np.full((devices, padded), -1, np.int64)
    rows[:, :pairs] = np.arange(devices * pairs).reshape(devices, pairs)
    return rows.reshape(-1)


def fermion_matrix(rows, count):
    n = np.arange(count, dtype=np.int64)
    angle = ((2 * n[None, :] - count + 1) * (2 * rows[:, None] + 1)) % (4 * count)
    angle = np.pi * angle / (2 * count)
    used = (rows >= 0)[:, None] * count**-0.5
    return np.concatenate([np.cos(angle) * used, np.sin(angle) * used], axis=0)


def boson_matrix(rows, count):
    v = np.arange(count, dtype=np.int64)
    angle = ((v[None, :] - count // 2) * (2 * rows[:, None] + 1)) % (2 * count)
    angle = np.pi * angle / count
    used = (rows >= 0)[:, None] * count**-0.5
    return np.concatenate([np.cos(angle) * used, np.sin(angle) * used], axis=0)


def plane_parts(side):
    p = np.arange(side * side, dtype=np.int64)
    angle = ((p[:, None] // side) * (p[None, :] // side) + (p[:, None] % side) * (p[None, :] % side)) % side
    angle = 2 * np.pi * angle / side
    scale = side**-1.5
    return np.cos(angle) * scale, np.sin(angle) * scale


def plane_matrix(side):
    cosine, sine = plane_parts(side)
    return np.block([[cosine, sine], [-sine, cosine]])


def times_w4(re, im, power, sign):
    power = (power * sign) % 4
    if power == 0:
        return re, im
    if power == 1:
        return -im, re
    if power == 2:
        return -re, -im
    return im, -re


def dft4(values, sign):
    (r0, i0), (r1, i1), (r2, i2), (r3, i3) = values
    sr, si, dr, di = r0 + r2, i0 + i2, r0 - r2, i0 - i2
    tr, ti, er, ei = r1 + r3, i1 + i3, r1 - r3, i1 - i3
    if sign > 0:
        return [(sr + tr, si + ti), (dr - ei, di + er), (sr - tr, si - ti), (dr + ei, di - er)]
    return [(sr + tr, si + ti), (dr + ei, di - er), (sr - tr, si - ti), (dr - ei, di + er)]


def twiddle(value, power, sign, side):
    re, im = value
    if power % (side // 4) == 0:
        return times_w4(re, im, power // (side // 4), sign)
    angle = 2.0 * np.pi * power / side
    c, s = float(np.cos(angle)), float(sign * np.sin(angle))
    return re * c - im * s, re * s + im * c


def dft_line(values, sign):
    side = len(values)
    if side == 1:
        return values
    if side == 2:
        (r0, i0), (r1, i1) = values
        return [(r0 + r1, i0 + i1), (r0 - r1, i0 - i1)]
    if side == 4:
        return dft4(values, sign)
    inner = side // 4
    parts = [dft_line(values[b::4], sign) for b in range(4)]
    out = [None] * side
    for k1 in range(inner):
        column = [twiddle(parts[b][k1], b * k1, sign, side) for b in range(4)]
        for k2, value in enumerate(dft4(column, sign)):
            out[k1 + inner * k2] = value
    return out


def times_kernel(g_ref, mh_ref, ml_ref, out_ref):
    lanes = g_ref.shape[2]
    groups, _, _, _, rows, _ = out_ref.shape
    half = groups * rows
    g = jnp.concatenate([g_ref[0, 0], g_ref[1, 0]], axis=0)
    d = dot3((mh_ref[...], ml_ref[...]), split_value(g), ((1,), (1,)))
    c_re, c_im = d[:half, :lanes], d[:half, lanes:]
    s_re, s_im = d[half:, :lanes], d[half:, lanes:]
    for where, value in (
        ((0, 0), c_re + s_im),
        ((0, 1), c_im - s_re),
        ((1, 0), s_im - c_re),
        ((1, 1), -(c_im + s_re)),
    ):
        out_ref[:, where[0], where[1], 0] = value.reshape(groups, rows, lanes)


def to_times(green, devices, padded, matrix):
    _, entries, lanes, count = green.shape
    return pl.pallas_call(
        times_kernel,
        grid=(entries,),
        in_specs=[
            pl.BlockSpec((2, 1, lanes, count), lambda e: (0, e, 0, 0)),
            pl.BlockSpec(matrix[0].shape, lambda e: (0, 0)),
            pl.BlockSpec(matrix[1].shape, lambda e: (0, 0)),
        ],
        out_specs=pl.BlockSpec((devices, 2, 2, 1, padded, lanes), lambda e: (0, 0, 0, e, 0, 0)),
        out_shape=jax.ShapeDtypeStruct((devices, 2, 2, entries, padded, lanes), jnp.float32),
        compiler_params=pltpu.CompilerParams(vmem_limit_bytes=32 << 20),
        name="to_times",
    )(green, *matrix)


def mirror_kernel(index_ref, ch_ref, cl_ref, sh_ref, sl_ref, fh_ref, fl_ref, bh_ref, bl_ref):
    plane = ch_ref.shape[0]
    row = lax.broadcasted_iota(jnp.int32, (plane, plane), 0)
    pick = (row == index_ref[...]).astype(jnp.float32).astype(jnp.bfloat16)

    def dot(a, b):
        return jnp.dot(a, b, preferred_element_type=jnp.float32)

    for c_ref, s_ref, f_ref, b_ref in ((ch_ref, sh_ref, fh_ref, bh_ref), (cl_ref, sl_ref, fl_ref, bl_ref)):
        cosine, sine = dot(c_ref[...], pick), dot(s_ref[...], pick)
        f_ref[:plane, :plane] = cosine.astype(jnp.bfloat16)
        f_ref[plane:, plane:] = cosine.astype(jnp.bfloat16)
        f_ref[:plane, plane:] = sine.astype(jnp.bfloat16)
        f_ref[plane:, :plane] = (-sine).astype(jnp.bfloat16)
        cosine, sine = dot(pick, c_ref[...]), dot(pick, s_ref[...])
        b_ref[:plane, :plane] = cosine.astype(jnp.bfloat16)
        b_ref[plane:, plane:] = cosine.astype(jnp.bfloat16)
        b_ref[:plane, plane:] = (-sine).astype(jnp.bfloat16)
        b_ref[plane:, :plane] = sine.astype(jnp.bfloat16)


def mirror_matrices(mirror_map, side):
    plane = side * side
    index = (mirror_map[1][:, None] * side + mirror_map[2][None, :]).reshape(1, plane)
    cosine, sine = plane_parts(side)
    parts = split_constant(cosine) + split_constant(sine)
    square = jax.ShapeDtypeStruct((2 * plane, 2 * plane), jnp.bfloat16)
    return pl.pallas_call(
        mirror_kernel,
        out_shape=[square] * 4,
        compiler_params=pltpu.CompilerParams(vmem_limit_bytes=32 << 20),
        name="mirror_matrices",
    )(index, *[jnp.asarray(part) for part in parts])


def space_kernel(x_ref, ph_ref, pl_ref, mh_ref, ml_ref, out_ref, mid):
    side, _, halves, _, entries, rows, lanes = x_ref.shape
    plane = 2 * lanes
    for half in range(halves):
        pieces = [
            x_ref[:, h, half, ri].reshape(side * entries * rows, lanes) for ri in range(2) for h in range(2)
        ]
        matrix = (ph_ref[...], pl_ref[...]) if half == 0 else (mh_ref[...], ml_ref[...])
        d = dot3(split_value(jnp.concatenate(pieces, axis=1)), matrix, ((1,), (0,)))
        for ri in range(2):
            mid[half, :, ri] = d[:, ri * plane : (ri + 1) * plane].reshape(side, entries, rows, plane)
    for half in range(halves):

        @pl.loop(0, entries)
        def _(e):
            for block in range(2):
                cut = pl.ds(block * lanes, lanes)
                values = [(mid[half, x, 0, e, :, cut], mid[half, x, 1, e, :, cut]) for x in range(side)]
                for x, (re, im) in enumerate(dft_line(values, 1)):
                    out_ref[half, x, 0, e, :, cut] = re
                    out_ref[half, x, 1, e, :, cut] = im


def to_space(x, plain, mirrored):
    side, _, halves, _, entries, rows, lanes = x.shape
    shape = (halves, side, 2, entries, rows, 2 * lanes)
    return pl.pallas_call(
        space_kernel,
        out_shape=jax.ShapeDtypeStruct(shape, jnp.float32),
        scratch_shapes=[pltpu.VMEM(shape, jnp.float32)],
        compiler_params=pltpu.CompilerParams(vmem_limit_bytes=40 << 20),
        name="to_space",
    )(x, *plain, *mirrored)


def bubble_kernel(first, table_ref, mirror_ref, g_ref, ph_ref, pl_ref, mh_ref, ml_ref, out_ref, mid):
    halves, side, _, _, rows, plane = g_ref.shape
    members = out_ref.shape[4]
    lanes = plane // 2

    @pl.loop(0, members)
    def _(c):
        left, right = table_ref[first + c, 0], table_ref[first + c, 1]
        for half in range(halves):
            for block in range(2):
                cut = pl.ds(block * lanes, lanes)
                values = []
                for x in range(side):
                    other = mirror_ref[0, x]
                    a_re = g_ref[half, x, 0, left, :, cut]
                    a_im = g_ref[half, x, 1, left, :, cut]
                    b_re = g_ref[1 - half, other, 0, right, :, cut]
                    b_im = g_ref[1 - half, other, 1, right, :, cut]
                    values.append((a_re * b_re - a_im * b_im, a_re * b_im + a_im * b_re))
                for x, (re, im) in enumerate(dft_line(values, -1)):
                    mid[half, x, c, 0, :, cut] = re
                    mid[half, x, c, 1, :, cut] = im

    for half in range(halves):
        matrix = (ph_ref[...], pl_ref[...]) if half == 0 else (mh_ref[...], ml_ref[...])
        count = side * members * rows
        value = jnp.concatenate([mid[half, :, :, ri].reshape(count, plane) for ri in range(2)], axis=1)
        d = dot3(split_value(value), matrix, ((1,), (0,)))
        for ri in range(2):
            for h in range(2):
                start = ri * plane + h * lanes
                out_ref[:, h, half, ri] = d[:, start : start + lanes].reshape(side, members, rows, lanes)


def bubbles(first, members, table, mirror_map, space, plain, mirrored):
    halves, side, _, _, rows, plane = space.shape
    smem = pl.BlockSpec(memory_space=pltpu.SMEM)
    vmem = pl.BlockSpec(memory_space=pltpu.VMEM)
    return pl.pallas_call(
        functools.partial(bubble_kernel, first),
        in_specs=[smem, smem] + [vmem] * 5,
        out_shape=jax.ShapeDtypeStruct((side, 2, halves, 2, members, rows, plane // 2), jnp.float32),
        scratch_shapes=[pltpu.VMEM((halves, side, members, 2, rows, plane), jnp.float32)],
        compiler_params=pltpu.CompilerParams(vmem_limit_bytes=48 << 20),
        name="bubbles",
    )(table, mirror_map, space, *plain, *mirrored)


def frequency_kernel(y_ref, mh_ref, ml_ref, *refs):
    out_ref = refs[-1]
    devices, _, _, _, rows, lanes = y_ref.shape
    count = devices * rows

    def part(half, ri):
        return y_ref[:, half, ri, 0].reshape(count, lanes)

    sums = [part(0, ri) + part(1, ri) for ri in range(2)]
    differences = [part(0, ri) - part(1, ri) for ri in range(2)]
    upper = jnp.concatenate([sums[0], -differences[1]], axis=0)
    lower = jnp.concatenate([sums[1], differences[0]], axis=0)
    value = jnp.concatenate([upper.T, lower.T], axis=0)
    d = dot3(split_value(value), (mh_ref[...], ml_ref[...]), ((1,), (0,)))
    out_ref[0, 0] = d[:lanes]
    out_ref[1, 0] = d[lanes:]


def to_frequencies(y, matrix, first, total, earlier):
    devices, _, _, members, rows, lanes = y.shape
    count = matrix[0].shape[1]
    whole = pl.BlockSpec(matrix[0].shape, lambda c: (0, 0))
    args = (y,) + tuple(matrix)
    specs = [pl.BlockSpec((devices, 2, 2, 1, rows, lanes), lambda c: (0, 0, 0, c, 0, 0)), whole, whole]
    aliases = {}
    if earlier is not None:
        args += (earlier,)
        specs.append(pl.BlockSpec(memory_space=pl.ANY))
        aliases = {3: 0}
    return pl.pallas_call(
        frequency_kernel,
        grid=(members,),
        in_specs=specs,
        out_specs=pl.BlockSpec((2, 1, lanes, count), lambda c: (0, first + c, 0, 0)),
        out_shape=jax.ShapeDtypeStruct((2, total, lanes, count), jnp.float32),
        input_output_aliases=aliases,
        compiler_params=pltpu.CompilerParams(vmem_limit_bytes=32 << 20),
        name="to_frequencies",
    )(*args)


def exchange(x):
    shape = x.shape
    flat = x.reshape(shape[0], -1, shape[-1])
    return lax.all_to_all(flat, "kb", split_axis=0, concat_axis=0, tiled=True).reshape(shape)


def local(green, pair_table, mirror_map):
    side = mirror_map.shape[1]
    plane = side * side
    lanes, count = green.shape[2], green.shape[3]
    devices = side * plane // lanes
    pairs = count // (2 * devices)
    padded = -(-pairs // ROWS) * ROWS
    strips = plane // 2 // lanes
    components = pair_table.shape[0]
    rows = time_rows(devices, pairs, padded)
    forward = [jnp.asarray(part) for part in split_constant(fermion_matrix(rows, count))]
    backward = [jnp.asarray(part) for part in split_constant(boson_matrix(rows, count))]
    flat = plane_matrix(side)
    plain = [jnp.asarray(part) for part in split_constant(flat)]
    plain_back = [jnp.asarray(part) for part in split_constant(flat.T)]

    def arrived(x):
        x = exchange(x[..., :pairs, :])
        x = jnp.pad(x, ((0, 0),) * 4 + ((0, padded - pairs), (0, 0)))
        x = x.reshape((side, 2, strips) + x.shape[1:])
        x = jnp.moveaxis(x, 2, -2)
        return x.reshape(x.shape[:-2] + (strips * lanes,))

    def returned(x):
        x = x[..., :pairs, :]
        x = x.reshape(x.shape[:-1] + (strips, lanes))
        x = jnp.moveaxis(x, -2, 2)
        x = exchange(x.reshape((devices,) + x.shape[3:]))
        return jnp.pad(x, ((0, 0),) * 4 + ((0, padded - pairs), (0, 0)))

    mirrored = mirror_matrices(mirror_map, side)
    space = to_space(arrived(to_times(green, devices, padded, forward)), plain, mirrored[:2])
    members = components // GROUPS
    out = None
    for group in range(GROUPS):
        first = group * members
        chi = bubbles(first, members, pair_table, mirror_map, space, plain_back, mirrored[2:])
        out = to_frequencies(returned(chi), backward, first, components, out)
    return out


def solution(mesh):
    placed = (P("set", None, "kb", None), P(), P("set", None))
    return jax.shard_map(
        local, mesh=mesh, in_specs=placed, out_specs=P("set", None, "kb", None), check_vma=False
    )
```

profile of v0, /device:TPU:0, one launch (start us, length us, event | category | flops | bytes accessed | tf_op | source)
XLA Modules:
  0.0 180.8 jit_solution(12781745693352700795)
XLA Ops:
  0.0 1.6 copy-done.1
  1.6 1.0 copy-done.16
  2.6 1.0 copy-done.17
  3.7 2.9 %to_times.1 = f32[32,2,2,4,8,128]{5,4,3,2,1,0:T(8,128)S(1)} custom-call(f32[2,4,128,512]{3,2,1,0:T(8,128)S(1)} %copy-done.1, bf16[512,512]{1,0:T(8,128)(2,1)S(1)} %copy-done.17, bf16[512,512]{1,0:T(8,128)(2,1)S(1)} %copy-done.16), custom_call_target="tpu_custom_call" | custom-call | tf_op jit(solution)/shard_map/to_times/pallas_call | solution.py:138
  6.6 0.0 copy-start
  6.6 1.3 copy-done
  7.9 0.0 copy-start.20
  7.9 0.0 copy-start.6
  7.9 0.0 copy-start.7
  7.9 7.3 %all-to-all-start = ((f32[32,128,128]{2,1,0:T(8,128)}), f32[32,128,128]{2,1,0:T(8,128)S(1)}, u32[]{:S(2)}, u32[]{:S(2)}) async-start(f32[32,128,128]{2,1,0:T(8,128)} %bitcast.10), calls=%async_computation | async-start | bytes 4194304 | tf_op jit(solution)/shard_map/all_to_all | solution.py:315
  15.2 0.0 copy-done.23
  15.3 0.1 copy.16.table_ref
  15.3 0.0 copy-done.22
  15.3 0.7 broadcast_add_fusion
  16.0 0.8 add.29.index_ref
  16.8 0.0 copy-done.18
  16.8 0.0 copy-done.19
  16.8 0.0 copy-done.20
  16.8 0.0 copy-start.21
  16.8 0.9 copy-done.21
  17.7 0.4 mirror_matrices.1
  18.2 0.8 copy-done.8
  19.0 0.8 copy-done.10
  19.8 0.8 copy-done.12
  20.6 0.8 copy-done.14
  21.4 42.8 %all-to-all-done = f32[32,128,128]{2,1,0:T(8,128)S(1)} async-done(((f32[32,128,128]{2,1,0:T(8,128)}), f32[32,128,128]{2,1,0:T(8,128)S(1)}, u32[]{:S(2)}, u32[]{:S(2)}) %all-to-all-start) | async-done | bytes 2097184 | tf_op jit(solution)/shard_map/all_to_all | solution.py:315
  64.2 1.0 copy-done.13
  65.2 1.0 copy-done.15
  66.2 2.4 %to_space.1.g_ref = f32[2,16,2,4,8,256]{5,4,3,2,1,0:T(8,128)S(1)} custom-call(f32[16,2,2,2,4,8,128]{6,5,4,3,2,1,0:T(8,128)S(1)} %bitcast.9, bf16[512,512]{1,0:T(8,128)(2,1)S(1)} %copy-done.7, bf16[512,512]{1,0:T(8,128)(2,1)S(1)} %copy-done.6, bf16[512,512]{1,0:T(8,128)(2,1)S(1)} %copy-done.13, bf16[512,512]{1,0:T(8,128)(2,1)S(1)} %copy-done.15), custom_call_target="tpu_custom_call" | custom-call | tf_op jit(solution)/shard_map/to_space/pallas_call | solution.py:214
  68.7 7.8 %bubbles.1 = f32[16,2,2,2,8,8,128]{6,5,4,3,2,1,0:T(8,128)} custom-call(s32[8,2]{1,0:T(8,128)S(1)} %copy.16.table_ref, s32[3,16]{1,0:T(4,128)S(1)} %copy-done.22, f32[2,16,2,4,8,256]{5,4,3,2,1,0:T(8,128)S(1)} %to_space.1.g_ref, bf16[512,512]{1,0:T(8,128)(2,1)S(1)} %copy-done.5, bf16[512,512]{1,0:T(8,128)(2,1)S(1)} %copy-done.4, ...), custom_call_target="tpu_custom_call" | custom-call | tf_op jit(solution)/shard_map/bubbles/pallas_call | solution.py:261
  76.4 97.7 %all_to_all.10 = f32[32,256,128]{2,1,0:T(8,128)S(1)} all-to-all(f32[32,256,128]{2,1,0:T(8,128)} %bitcast.11), channel_id=1, replica_groups=mesh['set'=1,'kb'=32] {'kb'}, dimensions={0} | all-to-all | bytes 8388608 | tf_op jit(solution)/shard_map/all_to_all | solution.py:315
  174.1 6.7 %to_frequencies.1 = f32[2,8,128,512]{3,2,1,0:T(8,128)} custom-call(f32[32,2,2,8,8,128]{5,4,3,2,1,0:T(8,128)S(1)} %bitcast.8, bf16[512,512]{1,0:T(8,128)(2,1)S(1)} %copy-done.3, bf16[512,512]{1,0:T(8,128)(2,1)S(1)} %copy-done.2), custom_call_target="tpu_custom_call" | custom-call | tf_op jit(solution)/shard_map/to_frequencies/pallas_call | solution.py:300
  (28 shorter events, 0.1 us)
Async XLA Ops:
  0.0 1.6 copy-start.1
  1.6 1.0 copy-start.16
  2.6 1.0 copy-start.17
  6.6 1.3 copy-start
  7.9 7.4 %copy-start.23 = (s32[8,2]{0,1:T(2,128)S(1)}, s32[8,2]{0,1:T(2,128)}, u32[]{:S(2)}) copy-start(s32[8,2]{0,1:T(2,128)} %param.16) | copy-start | bytes 196
  7.9 7.5 %copy-start.22 = (s32[3,16]{1,0:T(4,128)S(1)}, s32[3,16]{1,0:T(4,128)}, u32[]{:S(2)}) copy-start(s32[3,16]{1,0:T(4,128)} %mirror_ref.1) | copy-start | bytes 580
  7.9 8.9 %copy-start.18 = (bf16[256,256]{1,0:T(8,128)(2,1)S(1)}, bf16[256,256]{1,0:T(8,128)(2,1)}, u32[]{:S(2)}) copy-start(bf16[256,256]{1,0:T(8,128)(2,1)} %constant.38.clone.sl_ref) | copy-start | bytes 393220
  7.9 8.9 %copy-start.19 = (bf16[256,256]{1,0:T(8,128)(2,1)S(1)}, bf16[256,256]{1,0:T(8,128)(2,1)}, u32[]{:S(2)}) copy-start(bf16[256,256]{1,0:T(8,128)(2,1)} %constant.37.clone.sh_ref) | copy-start | bytes 393220
  7.9 8.9 %copy-start.20 = (bf16[256,256]{1,0:T(8,128)(2,1)S(1)}, bf16[256,256]{1,0:T(8,128)(2,1)}, u32[]{:S(2)}) copy-start(bf16[256,256]{1,0:T(8,128)(2,1)} %constant.36.clone.cl_ref) | copy-start | bytes 393220
  7.9 56.2 %copy-start.6 = (bf16[512,512]{1,0:T(8,128)(2,1)S(1)}, bf16[512,512]{1,0:T(8,128)(2,1)}, u32[]{:S(2)}) copy-start(bf16[512,512]{1,0:T(8,128)(2,1)} %constant.32.clone.pl_ref) | copy-start | bytes 1572868
  7.9 56.2 %copy-start.7 = (bf16[512,512]{1,0:T(8,128)(2,1)S(1)}, bf16[512,512]{1,0:T(8,128)(2,1)}, u32[]{:S(2)}) copy-start(bf16[512,512]{1,0:T(8,128)(2,1)} %constant.31.clone.ph_ref) | copy-start | bytes 1572868
  7.9 56.2 %all-to-all-start = ((f32[32,128,128]{2,1,0:T(8,128)}), f32[32,128,128]{2,1,0:T(8,128)S(1)}, u32[]{:S(2)}, u32[]{:S(2)}) async-start(f32[32,128,128]{2,1,0:T(8,128)} %bitcast.10), calls=%async_computation | async-start | bytes 4194304 | tf_op jit(solution)/shard_map/all_to_all | solution.py:315
  16.8 0.9 copy-start.21
  18.2 0.8 copy-start.8
  19.0 0.8 copy-start.10
  19.8 0.8 copy-start.12
  20.6 0.8 copy-start.14
  64.1 1.0 copy-start.13
  65.2 1.0 copy-start.15
  66.2 2.4 %copy-start.4 = (bf16[512,512]{1,0:T(8,128)(2,1)S(1)}, bf16[512,512]{1,0:T(8,128)(2,1)}, u32[]{:S(2)}) copy-start(bf16[512,512]{1,0:T(8,128)(2,1)} %constant.34.clone.pl_ref) | copy-start | bytes 1572868
  66.2 2.4 %copy-start.5 = (bf16[512,512]{1,0:T(8,128)(2,1)S(1)}, bf16[512,512]{1,0:T(8,128)(2,1)}, u32[]{:S(2)}) copy-start(bf16[512,512]{1,0:T(8,128)(2,1)} %constant.33.clone.ph_ref) | copy-start | bytes 1572868
  66.2 2.4 %copy-start.9 = (bf16[512,512]{1,0:T(8,128)(2,1)S(1)}, bf16[512,512]{1,0:T(8,128)(2,1)}, u32[]{:S(2)}) copy-start(bf16[512,512]{1,0:T(8,128)(2,1)} %copy-done.8) | copy-start | bytes 1572868
  66.2 2.4 %copy-start.11 = (bf16[512,512]{1,0:T(8,128)(2,1)S(1)}, bf16[512,512]{1,0:T(8,128)(2,1)}, u32[]{:S(2)}) copy-start(bf16[512,512]{1,0:T(8,128)(2,1)} %copy-done.10) | copy-start | bytes 1572868
  76.4 97.7 %copy-start.2 = (bf16[512,512]{1,0:T(8,128)(2,1)S(1)}, bf16[512,512]{1,0:T(8,128)(2,1)}, u32[]{:S(2)}) copy-start(bf16[512,512]{1,0:T(8,128)(2,1)} %constant.30.clone.ml_ref) | copy-start | bytes 1572868
  76.4 97.7 %copy-start.3 = (bf16[512,512]{1,0:T(8,128)(2,1)S(1)}, bf16[512,512]{1,0:T(8,128)(2,1)}, u32[]{:S(2)}) copy-start(bf16[512,512]{1,0:T(8,128)(2,1)} %constant.29.clone.mh_ref) | copy-start | bytes 1572868
where the time goes:
time: 181 us
  blocking collectives  97.7 us (54%)
  waiting for transfers between devices  42.8 us (24%)
  Pallas kernels  20.2 us (11%)
  local copies, waits for them, and re-layouts  12.1 us (7%)
  starting transfers between devices  7.3 us (4%)
    all_to_all x1, blocking collectives, exchange(): lax.all_to_all(flat, 'kb', split_axis=0, concat_axis=0, tiled=True)  97.7 us
    all_to_all x1, waiting for transfers between devices, exchange(): lax.all_to_all(flat, 'kb', split_axis=0, concat_axis=0, tiled=True)  42.8 us
    unnamed x49, local copies, waits for them, and re-layouts  11.3 us
    pallas_call x1, Pallas kernels, bubbles(): pl.pallas_call(functools.partial(bubble_kernel, first), in_specs=[smem, s...  7.77 us
    all_to_all x1, starting transfers between devices, exchange(): lax.all_to_all(flat, 'kb', split_axis=0, concat_axis=0, tiled=True)  7.3 us
    pallas_call x1, Pallas kernels, to_frequencies(): pl.pallas_call(frequency_kernel, grid=(members,), in_specs=specs, out_spe...  6.72 us
  transfers between devices with their start and end apart: 1, of which 1 were waited for; matrix products, arithmetic and copies ran while one was open for 1% of the time, Pallas kernels for 0%

commit v1 on v0

v1 whole, which is shorter than its diff:
```python
import jax
import jax.numpy as jnp
import ml_dtypes
import numpy as np
from jax import lax
from jax.experimental import pallas as pl
from jax.experimental.pallas import tpu as pltpu
from jax.sharding import PartitionSpec as P

LANES = 128
ROWS = 8
GROUPS = 2


def split_constant(matrix):
    high = matrix.astype(np.float32).astype(ml_dtypes.bfloat16)
    low = (matrix - high.astype(np.float64)).astype(np.float32).astype(ml_dtypes.bfloat16)
    return high, low


def split_value(value):
    high = value.astype(jnp.bfloat16)
    low = (value - high.astype(jnp.float32)).astype(jnp.bfloat16)
    return high, low


def dot3(left, right, dims):
    def one(a, b):
        return lax.dot_general(a, b, (dims, ((), ())), preferred_element_type=jnp.float32)

    return one(left[0], right[0]) + (one(left[0], right[1]) + one(left[1], right[0]))


def time_rows(devices, pairs, padded):
    rows = np.full((devices, padded), -1, np.int64)
    rows[:, :pairs] = np.arange(devices * pairs).reshape(devices, pairs)
    return rows.reshape(-1)


def fermion_matrix(rows, count):
    n = np.arange(count, dtype=np.int64)
    angle = ((2 * n[None, :] - count + 1) * (2 * rows[:, None] + 1)) % (4 * count)
    angle = np.pi * angle / (2 * count)
    used = (rows >= 0)[:, None] * count**-0.5
    return np.concatenate([np.cos(angle) * used, np.sin(angle) * used], axis=0)


def boson_matrix(rows, count):
    v = np.arange(count, dtype=np.int64)
    angle = ((v[None, :] - count // 2) * (2 * rows[:, None] + 1)) % (2 * count)
    angle = np.pi * angle / count
    used = (rows >= 0)[:, None] * count**-0.5
    return np.concatenate([np.cos(angle) * used, np.sin(angle) * used], axis=0)


def plane_parts(side):
    p = np.arange(side * side, dtype=np.int64)
    angle = ((p[:, None] // side) * (p[None, :] // side) + (p[:, None] % side) * (p[None, :] % side)) % side
    angle = 2 * np.pi * angle / side
    scale = side**-1.5
    return np.cos(angle) * scale, np.sin(angle) * scale


def times_w4(re, im, power, sign):
    power = (power * sign) % 4
    if power == 0:
        return re, im
    if power == 1:
        return -im, re
    if power == 2:
        return -re, -im
    return im, -re


def dft4(values, sign):
    (r0, i0), (r1, i1), (r2, i2), (r3, i3) = values
    sr, si, dr, di = r0 + r2, i0 + i2, r0 - r2, i0 - i2
    tr, ti, er, ei = r1 + r3, i1 + i3, r1 - r3, i1 - i3
    if sign > 0:
        return [(sr + tr, si + ti), (dr - ei, di + er), (sr - tr, si - ti), (dr + ei, di - er)]
    return [(sr + tr, si + ti), (dr + ei, di - er), (sr - tr, si - ti), (dr - ei, di + er)]


def twiddle(value, power, sign, side):
    re, im = value
    if power % (side // 4) == 0:
        return times_w4(re, im, power // (side // 4), sign)
    angle = 2.0 * np.pi * power / side
    c, s = float(np.cos(angle)), float(sign * np.sin(angle))
    return re * c - im * s, re * s + im * c


def dft_line(values, sign):
    side = len(values)
    if side == 1:
        return values
    if side == 2:
        (r0, i0), (r1, i1) = values
        return [(r0 + r1, i0 + i1), (r0 - r1, i0 - i1)]
    if side == 4:
        return dft4(values, sign)
    inner = side // 4
    parts = [dft_line(values[b::4], sign) for b in range(4)]
    out = [None] * side
    for k1 in range(inner):
        column = [twiddle(parts[b][k1], b * k1, sign, side) for b in range(4)]
        for k2, value in enumerate(dft4(column, sign)):
            out[k1 + inner * k2] = value
    return out


def times_kernel(g_ref, mh_ref, ml_ref, out_ref):
    lanes = g_ref.shape[2]
    groups, _, _, _, rows, _ = out_ref.shape
    half = groups * rows
    g = jnp.concatenate([g_ref[0, 0], g_ref[1, 0]], axis=0)
    d = dot3((mh_ref[...], ml_ref[...]), split_value(g), ((1,), (1,)))
    c_re, c_im = d[:half, :lanes], d[:half, lanes:]
    s_re, s_im = d[half:, :lanes], d[half:, lanes:]
    for where, value in (
        ((0, 0), c_re + s_im),
        ((0, 1), c_im - s_re),
        ((1, 0), s_im - c_re),
        ((1, 1), -(c_im + s_re)),
    ):
        out_ref[:, where[0], where[1], 0] = value.reshape(groups, rows, lanes)


def to_times(green, devices, padded, matrix):
    _, entries, lanes, count = green.shape
    return pl.pallas_call(
        times_kernel,
        grid=(entries,),
        in_specs=[
            pl.BlockSpec((2, 1, lanes, count), lambda e: (0, e, 0, 0)),
            pl.BlockSpec(matrix[0].shape, lambda e: (0, 0)),
            pl.BlockSpec(matrix[1].shape, lambda e: (0, 0)),
        ],
        out_specs=pl.BlockSpec((devices, 2, 2, 1, padded, lanes), lambda e: (0, 0, 0, e, 0, 0)),
        out_shape=jax.ShapeDtypeStruct((devices, 2, 2, entries, padded, lanes), jnp.float32),
        compiler_params=pltpu.CompilerParams(vmem_limit_bytes=60 << 20),
        name="to_times",
    )(green, *matrix)


def fill_block(ref, cosine, sine):
    plane = cosine.shape[0]
    ref[:plane, :plane] = cosine.astype(jnp.bfloat16)
    ref[plane:, plane:] = cosine.astype(jnp.bfloat16)
    ref[:plane, plane:] = sine.astype(jnp.bfloat16)
    ref[plane:, :plane] = (-sine).astype(jnp.bfloat16)


def middle_kernel(
    table_ref, mirror_ref, index_ref, x_ref, ch_ref, cl_ref, sh_ref, sl_ref, out_ref,
    forward, backward, mid, space, chi, stage, sems,
):
    side, _, halves, _, entries, rows, lanes = x_ref.shape
    plane = 2 * lanes
    units, _, _, _, members, _, _ = stage.shape
    row = lax.broadcasted_iota(jnp.int32, (plane, plane), 0)
    pick = (row == index_ref[...]).astype(jnp.float32).astype(jnp.bfloat16)

    def dot(a, b):
        return jnp.dot(a, b, preferred_element_type=jnp.float32)

    for part, (c_ref, s_ref) in enumerate(((ch_ref, sh_ref), (cl_ref, sl_ref))):
        cosine, sine = c_ref[...].astype(jnp.float32), s_ref[...].astype(jnp.float32)
        fill_block(forward.at[0, part], cosine, sine)
        fill_block(backward.at[0, part], cosine, -sine)
        fill_block(forward.at[1, part], dot(c_ref[...], pick), dot(s_ref[...], pick))
        fill_block(backward.at[1, part], dot(pick, c_ref[...]), -dot(pick, s_ref[...]))

    for half in range(halves):
        pieces = [
            x_ref[:, h, half, ri].reshape(side * entries * rows, lanes) for ri in range(2) for h in range(2)
        ]
        value = split_value(jnp.concatenate(pieces, axis=1))
        d = dot3(value, (forward[half, 0], forward[half, 1]), ((1,), (0,)))
        for ri in range(2):
            mid[half, :, ri] = d[:, ri * plane : (ri + 1) * plane].reshape(side, entries, rows, plane)
    for half in range(halves):
        for e in range(entries):
            for block in range(2):
                cut = slice(block * lanes, (block + 1) * lanes)
                values = [(mid[half, x, 0, e, :, cut], mid[half, x, 1, e, :, cut]) for x in range(side)]
                for x, (re, im) in enumerate(dft_line(values, 1)):
                    space[half, x, 0, e, :, cut] = re
                    space[half, x, 1, e, :, cut] = im

    copies = []
    for unit in range(units):
        half, first = unit % halves, unit // halves * members
        for c in range(members):
            left, right = table_ref[first + c, 0], table_ref[first + c, 1]
            for block in range(2):
                cut = slice(block * lanes, (block + 1) * lanes)
                values = []
                for x in range(side):
                    other = mirror_ref[0, x]
                    a_re = space[half, x, 0, left, :, cut]
                    a_im = space[half, x, 1, left, :, cut]
                    b_re = space[1 - half, other, 0, right, :, cut]
                    b_im = space[1 - half, other, 1, right, :, cut]
                    values.append((a_re * b_re - a_im * b_im, a_re * b_im + a_im * b_re))
                for x, (re, im) in enumerate(dft_line(values, -1)):
                    chi[unit, 0, x, c, :, cut] = re
                    chi[unit, 1, x, c, :, cut] = im
        count = side * members * rows
        value = jnp.concatenate([chi[unit, ri].reshape(count, plane) for ri in range(2)], axis=1)
        d = dot3(split_value(value), (backward[half, 0], backward[half, 1]), ((1,), (0,)))
        for ri in range(2):
            for h in range(2):
                start = ri * plane + h * lanes
                stage[unit, :, h, ri] = d[:, start : start + lanes].reshape(side, members, rows, lanes)
        target = out_ref.at[:, :, half, :, pl.ds(first, members)]
        copies.append(pltpu.make_async_copy(stage.at[unit], target, sems.at[unit]))
        copies[-1].start()
    for copy in copies:
        copy.wait()


def middle(x, table, mirror_map):
    side, _, halves, _, entries, rows, lanes = x.shape
    plane = 2 * lanes
    components = table.shape[0]
    members = components // GROUPS
    units = halves * GROUPS
    index = (mirror_map[1][:, None] * side + mirror_map[2][None, :]).reshape(1, plane)
    cosine, sine = plane_parts(side)
    parts = [jnp.asarray(part) for part in split_constant(cosine) + split_constant(sine)]
    smem = pl.BlockSpec(memory_space=pltpu.SMEM)
    vmem = pl.BlockSpec(memory_space=pltpu.VMEM)
    matrices = pltpu.VMEM((halves, 2, 2 * plane, 2 * plane), jnp.bfloat16)
    spatial = pltpu.VMEM((halves, side, 2, entries, rows, plane), jnp.float32)
    return pl.pallas_call(
        middle_kernel,
        in_specs=[smem, smem] + [vmem] * 6,
        out_specs=pl.BlockSpec(memory_space=pltpu.HBM),
        out_shape=jax.ShapeDtypeStruct((side, 2, halves, 2, components, rows, lanes), jnp.float32),
        scratch_shapes=[
            matrices,
            matrices,
            spatial,
            spatial,
            pltpu.VMEM((units, 2, side, members, rows, plane), jnp.float32),
            pltpu.VMEM((units, side, 2, 2, members, rows, lanes), jnp.float32),
            pltpu.SemaphoreType.DMA((units,)),
        ],
        compiler_params=pltpu.CompilerParams(vmem_limit_bytes=48 << 20),
        name="middle",
    )(table, mirror_map, index, x, *parts)


def frequency_kernel(y_ref, mh_ref, ml_ref, out_ref, stage, sems):
    devices, _, _, components, rows, lanes = y_ref.shape
    count = devices * rows
    groups = sems.shape[0]
    members = components // groups
    matrix = (mh_ref[...], ml_ref[...])
    copies = []
    for group in range(groups):
        pieces = []
        for c in range(group * members, (group + 1) * members):
            part = [[y_ref[:, half, ri, c].reshape(count, lanes) for ri in range(2)] for half in range(2)]
            sums = [part[0][ri] + part[1][ri] for ri in range(2)]
            differences = [part[0][ri] - part[1][ri] for ri in range(2)]
            pieces.append(jnp.concatenate([sums[0], -differences[1]], axis=0).T)
            pieces.append(jnp.concatenate([sums[1], differences[0]], axis=0).T)
        d = dot3(split_value(jnp.concatenate(pieces, axis=0)), matrix, ((1,), (0,)))
        d = d.reshape(members, 2, lanes, d.shape[1])
        for ri in range(2):
            stage[ri, group * members : (group + 1) * members] = d[:, ri]
        cut = pl.ds(group * members, members)
        copies.append(pltpu.make_async_copy(stage.at[:, cut], out_ref.at[:, cut], sems.at[group]))
        copies[-1].start()
    for copy in copies:
        copy.wait()


def to_frequencies(y, matrix):
    components, lanes = y.shape[3], y.shape[5]
    shape = (2, components, lanes, matrix[0].shape[1])
    vmem = pl.BlockSpec(memory_space=pltpu.VMEM)
    return pl.pallas_call(
        frequency_kernel,
        in_specs=[vmem] * 3,
        out_specs=pl.BlockSpec(memory_space=pltpu.HBM),
        out_shape=jax.ShapeDtypeStruct(shape, jnp.float32),
        scratch_shapes=[pltpu.VMEM(shape, jnp.float32), pltpu.SemaphoreType.DMA((components // 2,))],
        compiler_params=pltpu.CompilerParams(vmem_limit_bytes=40 << 20),
        name="to_frequencies",
    )(y, *matrix)


def exchange(x):
    shape = x.shape
    flat = x.reshape(shape[0], -1, shape[-1])
    return lax.all_to_all(flat, "kb", split_axis=0, concat_axis=0, tiled=True).reshape(shape)


def local(green, pair_table, mirror_map):
    side = mirror_map.shape[1]
    plane = side * side
    lanes, count = green.shape[2], green.shape[3]
    devices = side * plane // lanes
    pairs = count // (2 * devices)
    padded = -(-pairs // ROWS) * ROWS
    strips = plane // 2 // lanes
    rows = time_rows(devices, pairs, padded)
    forward = [jnp.asarray(part) for part in split_constant(fermion_matrix(rows, count))]
    backward = [jnp.asarray(part) for part in split_constant(boson_matrix(rows, count))]

    def arrived(x):
        x = exchange(x[..., :pairs, :])
        x = jnp.pad(x, ((0, 0),) * 4 + ((0, padded - pairs), (0, 0)))
        x = x.reshape((side, 2, strips) + x.shape[1:])
        x = jnp.moveaxis(x, 2, -2)
        return x.reshape(x.shape[:-2] + (strips * lanes,))

    def returned(x):
        x = x[..., :pairs, :]
        x = x.reshape(x.shape[:-1] + (strips, lanes))
        x = jnp.moveaxis(x, -2, 2)
        x = exchange(x.reshape((devices,) + x.shape[3:]))
        return jnp.pad(x, ((0, 0),) * 4 + ((0, padded - pairs), (0, 0)))

    chi = middle(arrived(to_times(green, devices, padded, forward)), pair_table, mirror_map)
    return to_frequencies(returned(chi), backward)


def solution(mesh):
    placed = (P("set", None, "kb", None), P(), P("set", None))
    return jax.shard_map(
        local, mesh=mesh, in_specs=placed, out_specs=P("set", None, "kb", None), check_vma=False
    )
```

time: 181 us -> 174 us (0.961)
  local copies, waits for them, and re-layouts: 12.1 us -> 0.2 us
  waiting for transfers between devices: 42.8 us -> 48.6 us
    unnamed x49 -> x17, local copies, waits for them, and re-layouts: 11.3 us -> 0.12 us
    all_to_all x1, waiting for transfers between devices: 42.8 us -> 48.6 us  [exchange(): lax.all_to_all(flat, 'kb', split_axis=0, concat_axis=0, tiled=True)]
    pallas_call x4 -> x2, Pallas kernels: 17.3 us -> 14.8 us  [the longest x1 10.3 us: middle(): pl.pallas_call(middle_kernel, in_specs=[smem, smem] + [vmem] * 6, out_spe...]
    pallas_call x1, Pallas kernels: 2.88 us -> 5.41 us  [to_times(): pl.pallas_call(times_kernel, grid=(entries,), in_specs=[pl.BlockSpec((2,...]
  transfers between devices with their start and end apart: 1 -> 1, of which waited for: 1 -> 1; matrix products, arithmetic and copies ran while one was open for 1% -> 0% of each run, Pallas kernels for 0% -> 0%
where the time goes in v1:
time: 174 us
  blocking collectives  97.7 us (56%)
  waiting for transfers between devices  48.6 us (28%)
  Pallas kernels  20.2 us (12%)
  starting transfers between devices  7.34 us (4%)
    all_to_all x1, blocking collectives, exchange(): lax.all_to_all(flat, 'kb', split_axis=0, concat_axis=0, tiled=True)  97.7 us
    all_to_all x1, waiting for transfers between devices, exchange(): lax.all_to_all(flat, 'kb', split_axis=0, concat_axis=0, tiled=True)  48.6 us
    pallas_call x1, Pallas kernels, middle(): pl.pallas_call(middle_kernel, in_specs=[smem, smem] + [vmem] * 6, out_spe...  10.3 us
    all_to_all x1, starting transfers between devices, exchange(): lax.all_to_all(flat, 'kb', split_axis=0, concat_axis=0, tiled=True)  7.34 us
    pallas_call x1, Pallas kernels, to_times(): pl.pallas_call(times_kernel, grid=(entries,), in_specs=[pl.BlockSpec((2,...  5.41 us
    pallas_call x1, Pallas kernels, to_frequencies(): pl.pallas_call(frequency_kernel, in_specs=[vmem] * 3, out_specs=pl.BlockS...  4.5 us
  transfers between devices with their start and end apart: 1, of which 1 were waited for; matrix products, arithmetic and copies ran while one was open for 0% of the time, Pallas kernels for 0%

profile of v1, /device:TPU:0, one launch (start us, length us, event | category | flops | bytes accessed | tf_op | source)
XLA Modules:
  0.0 174.2 jit_solution(11894913710331389382)
XLA Ops:
  0.0 0.0 copy-start.2
  0.0 0.0 copy-start.3
  0.0 0.0 copy-start.4
  0.0 0.0 copy-start.5
  0.0 0.0 copy-start.7
  0.0 0.0 copy-start.6
  0.0 5.4 %to_times.1 = f32[32,2,2,4,8,128]{5,4,3,2,1,0:T(8,128)} custom-call(f32[2,4,128,512]{3,2,1,0:T(8,128)} %g_ref.1, bf16[512,512]{1,0:T(8,128)(2,1)} %constant.8.clone.mh_ref, bf16[512,512]{1,0:T(8,128)(2,1)} %constant.20.clone.ml_ref), custom_call_target="tpu_custom_call" | custom-call | tf_op jit(solution)/shard_map/to_times/pallas_call | solution.py:131
  5.4 7.3 %all-to-all-start = ((f32[32,128,128]{2,1,0:T(8,128)}), f32[32,128,128]{2,1,0:T(8,128)S(1)}, u32[]{:S(2)}, u32[]{:S(2)}) async-start(f32[32,128,128]{2,1,0:T(8,128)} %bitcast.11), calls=%async_computation | async-start | bytes 4194304 | tf_op jit(solution)/shard_map/all_to_all | solution.py:299
  12.8 0.0 copy-done.7
  12.8 0.1 copy.12.table_ref
  12.9 0.0 copy-done.6
  12.9 0.1 broadcast_add_fusion
  13.0 0.1 add.29.index_ref
  13.0 48.6 %all-to-all-done = f32[32,128,128]{2,1,0:T(8,128)S(1)} async-done(((f32[32,128,128]{2,1,0:T(8,128)}), f32[32,128,128]{2,1,0:T(8,128)S(1)}, u32[]{:S(2)}, u32[]{:S(2)}) %all-to-all-start) | async-done | bytes 2097184 | tf_op jit(solution)/shard_map/all_to_all | solution.py:299
  61.7 0.0 copy-done.2
  61.7 0.0 copy-done.3
  61.7 0.0 copy-done.4
  61.7 0.0 copy-done.5
  61.7 10.3 %middle.1 = f32[16,2,2,2,8,8,128]{6,5,4,3,2,1,0:T(8,128)} custom-call(s32[8,2]{1,0:T(8,128)S(1)} %copy.12.table_ref, s32[3,16]{1,0:T(4,128)S(1)} %copy-done.6, s32[1,256]{1,0:T(1,128)S(1)} %add.29.index_ref, f32[16,2,2,2,4,8,128]{6,5,4,3,2,1,0:T(8,128)S(1)} %bitcast.9, bf16[256,256]{1,0:T(8,128)(2,1)S(1)} %copy-done.5, bf16[256,256]{1,0:T(8,128)(2,1)S(1)} %copy-done.4, ...), custom_call_target="tpu_custom_call" | custom-call | tf_op jit(solution)/shard_map/middle/pallas_call | solution.py:236
  72.0 0.0 copy-start
  72.0 0.0 copy-start.1
  72.0 97.7 %all_to_all.10 = f32[32,256,128]{2,1,0:T(8,128)S(1)} all-to-all(f32[32,256,128]{2,1,0:T(8,128)} %bitcast.10), channel_id=1, replica_groups=mesh['set'=1,'kb'=32] {'kb'}, dimensions={0} | all-to-all | bytes 8388608 | tf_op jit(solution)/shard_map/all_to_all | solution.py:299
  169.7 0.0 copy-done
  169.7 0.0 copy-done.1
  169.7 4.5 %to_frequencies.1 = f32[2,8,128,512]{3,2,1,0:T(8,128)} custom-call(f32[32,2,2,8,8,128]{5,4,3,2,1,0:T(8,128)S(1)} %bitcast.8, bf16[512,512]{1,0:T(8,128)(2,1)S(1)} %copy-done.1, bf16[512,512]{1,0:T(8,128)(2,1)S(1)} %copy-done), custom_call_target="tpu_custom_call" | custom-call | tf_op jit(solution)/shard_map/to_frequencies/pallas_call | solution.py:285
  (1 shorter events, 0.0 us)
Async XLA Ops:
  0.0 61.7 %copy-start.2 = (bf16[256,256]{1,0:T(8,128)(2,1)S(1)}, bf16[256,256]{1,0:T(8,128)(2,1)}, u32[]{:S(2)}) copy-start(bf16[256,256]{1,0:T(8,128)(2,1)} %constant.26.clone.sl_ref) | copy-start | bytes 393220
  0.0 61.7 %copy-start.3 = (bf16[256,256]{1,0:T(8,128)(2,1)S(1)}, bf16[256,256]{1,0:T(8,128)(2,1)}, u32[]{:S(2)}) copy-start(bf16[256,256]{1,0:T(8,128)(2,1)} %constant.25.clone.sh_ref) | copy-start | bytes 393220
  0.0 61.7 %copy-start.4 = (bf16[256,256]{1,0:T(8,128)(2,1)S(1)}, bf16[256,256]{1,0:T(8,128)(2,1)}, u32[]{:S(2)}) copy-start(bf16[256,256]{1,0:T(8,128)(2,1)} %constant.24.clone.cl_ref) | copy-start | bytes 393220
  0.0 61.7 %copy-start.5 = (bf16[256,256]{1,0:T(8,128)(2,1)S(1)}, bf16[256,256]{1,0:T(8,128)(2,1)}, u32[]{:S(2)}) copy-start(bf16[256,256]{1,0:T(8,128)(2,1)} %constant.23.clone.ch_ref) | copy-start | bytes 393220
  0.0 12.8 %copy-start.7 = (s32[8,2]{0,1:T(2,128)S(1)}, s32[8,2]{0,1:T(2,128)}, u32[]{:S(2)}) copy-start(s32[8,2]{0,1:T(2,128)} %param.12) | copy-start | bytes 196
  0.0 12.9 %copy-start.6 = (s32[3,16]{1,0:T(4,128)S(1)}, s32[3,16]{1,0:T(4,128)}, u32[]{:S(2)}) copy-start(s32[3,16]{1,0:T(4,128)} %mirror_ref.1) | copy-start | bytes 580
  5.4 56.2 %all-to-all-start = ((f32[32,128,128]{2,1,0:T(8,128)}), f32[32,128,128]{2,1,0:T(8,128)S(1)}, u32[]{:S(2)}, u32[]{:S(2)}) async-start(f32[32,128,128]{2,1,0:T(8,128)} %bitcast.11), calls=%async_computation | async-start | bytes 4194304 | tf_op jit(solution)/shard_map/all_to_all | solution.py:299
  72.0 97.7 %copy-start = (bf16[512,512]{1,0:T(8,128)(2,1)S(1)}, bf16[512,512]{1,0:T(8,128)(2,1)}, u32[]{:S(2)}) copy-start(bf16[512,512]{1,0:T(8,128)(2,1)} %constant.22.clone.ml_ref) | copy-start | bytes 1572868
  72.0 97.7 %copy-start.1 = (bf16[512,512]{1,0:T(8,128)(2,1)S(1)}, bf16[512,512]{1,0:T(8,128)(2,1)}, u32[]{:S(2)}) copy-start(bf16[512,512]{1,0:T(8,128)(2,1)} %constant.21.clone.mh_ref) | copy-start | bytes 1572868

commit v2 on v1

--- a/solution.py
+++ b/solution.py
@@ -25,10 +25,10 @@
 
 
 def dot3(left, right, dims):
-    def one(a, b):
-        return lax.dot_general(a, b, (dims, ((), ())), preferred_element_type=jnp.float32)
-
-    return one(left[0], right[0]) + (one(left[0], right[1]) + one(left[1], right[0]))
+    (k_left,), (k_right,) = dims
+    a = jnp.concatenate([left[0], left[0], left[1]], axis=k_left)
+    b = jnp.concatenate([right[0], right[1], right[0]], axis=k_right)
+    return lax.dot_general(a, b, (dims, ((), ())), preferred_element_type=jnp.float32)
 
 
 def time_rows(devices, pairs, padded):
@@ -109,46 +109,78 @@
     return out
 
 
-def times_kernel(g_ref, mh_ref, ml_ref, out_ref):
-    lanes = g_ref.shape[2]
-    groups, _, _, _, rows, _ = out_ref.shape
+def times_kernel(g_hbm, mh_hbm, ml_hbm, out_ref, g_ref, mh_ref, ml_ref, stage, in_sems, m_sems, out_sems):
+    entries, lanes = g_ref.shape[1:3]
+    groups, _, _, _, rows, _ = stage.shape
     half = groups * rows
-    g = jnp.concatenate([g_ref[0, 0], g_ref[1, 0]], axis=0)
-    d = dot3((mh_ref[...], ml_ref[...]), split_value(g), ((1,), (1,)))
-    c_re, c_im = d[:half, :lanes], d[:half, lanes:]
-    s_re, s_im = d[half:, :lanes], d[half:, lanes:]
-    for where, value in (
-        ((0, 0), c_re + s_im),
-        ((0, 1), c_im - s_re),
-        ((1, 0), s_im - c_re),
-        ((1, 1), -(c_im + s_re)),
-    ):
-        out_ref[:, where[0], where[1], 0] = value.reshape(groups, rows, lanes)
+    loads = [
+        pltpu.make_async_copy(mh_hbm, mh_ref, m_sems.at[0]),
+        pltpu.make_async_copy(ml_hbm, ml_ref, m_sems.at[1]),
+    ]
+    pieces = [
+        pltpu.make_async_copy(g_hbm.at[:, pl.ds(e, 1)], g_ref.at[:, pl.ds(e, 1)], in_sems.at[e])
+        for e in range(entries)
+    ]
+    for copy in [pieces[0]] + loads + pieces[1:]:
+        copy.start()
+    for copy in loads:
+        copy.wait()
+    matrix = (mh_ref[...], ml_ref[...])
+    copies = []
+    for e in range(entries):
+        pieces[e].wait()
+        g = jnp.concatenate([g_ref[0, e], g_ref[1, e]], axis=0)
+        d = dot3(matrix, split_value(g), ((1,), (1,)))
+        c_re, c_im = d[:half, :lanes], d[:half, lanes:]
+        s_re, s_im = d[half:, :lanes], d[half:, lanes:]
+        for where, value in (
+            ((0, 0), c_re + s_im),
+            ((0, 1), c_im - s_re),
+            ((1, 0), s_im - c_re),
+            ((1, 1), -(c_im + s_re)),
+        ):
+            stage[:, where[0], where[1], e] = value.reshape(groups, rows, lanes)
+        cut = pl.ds(e, 1)
+        copies.append(pltpu.make_async_copy(stage.at[:, :, :, cut], out_ref.at[:, :, :, cut], out_sems.at[e]))
+        copies[-1].start()
+    for copy in copies:
+        copy.wait()
 
 
 def to_times(green, devices, padded, matrix):
     _, entries, lanes, count = green.shape
+    shape = (devices, 2, 2, entries, padded, lanes)
+    hbm = pl.BlockSpec(memory_space=pltpu.HBM)
     return pl.pallas_call(
         times_kernel,
-        grid=(entries,),
-        in_specs=[
-            pl.BlockSpec((2, 1, lanes, count), lambda e: (0, e, 0, 0)),
-            pl.BlockSpec(matrix[0].shape, lambda e: (0, 0)),
-            pl.BlockSpec(matrix[1].shape, lambda e: (0, 0)),
+        in_specs=[hbm] * 3,
+        out_specs=hbm,
+        out_shape=jax.ShapeDtypeStruct(shape, jnp.float32),
+        scratch_shapes=[
+            pltpu.VMEM(green.shape, jnp.float32),
+            pltpu.VMEM(matrix[0].shape, jnp.bfloat16),
+            pltpu.VMEM(matrix[1].shape, jnp.bfloat16),
+            pltpu.VMEM(shape, jnp.float32),
+            pltpu.SemaphoreType.DMA((entries,)),
+            pltpu.SemaphoreType.DMA((2,)),
+            pltpu.SemaphoreType.DMA((entries,)),
         ],
-        out_specs=pl.BlockSpec((devices, 2, 2, 1, padded, lanes), lambda e: (0, 0, 0, e, 0, 0)),
-        out_shape=jax.ShapeDtypeStruct((devices, 2, 2, entries, padded, lanes), jnp.float32),
-        compiler_params=pltpu.CompilerParams(vmem_limit_bytes=60 << 20),
+        compiler_params=pltpu.CompilerParams(vmem_limit_bytes=32 << 20),
         name="to_times",
     )(green, *matrix)
 
 
 def fill_block(ref, cosine, sine):
     plane = cosine.shape[0]
-    ref[:plane, :plane] = cosine.astype(jnp.bfloat16)
-    ref[plane:, plane:] = cosine.astype(jnp.bfloat16)
-    ref[:plane, plane:] = sine.astype(jnp.bfloat16)
-    ref[plane:, :plane] = (-sine).astype(jnp.bfloat16)
+    lanes = plane // 2
+    for block in range(2):
+        cut = slice(block * lanes, (block + 1) * lanes)
+        re = slice(2 * block * lanes, (2 * block + 1) * lanes)
+        im = slice((2 * block + 1) * lanes, (2 * block + 2) * lanes)
+        ref[:plane, re] = cosine[:, cut].astype(jnp.bfloat16)
+        ref[plane:, im] = cosine[:, cut].astype(jnp.bfloat16)
+        ref[:plane, im] = sine[:, cut].astype(jnp.bfloat16)
+        ref[plane:, re] = (-sine[:, cut]).astype(jnp.bfloat16)
 
 
 def middle_kernel(
@@ -171,51 +203,81 @@
         fill_block(forward.at[1, part], dot(c_ref[...], pick), dot(s_ref[...], pick))
         fill_block(backward.at[1, part], dot(pick, c_ref[...]), -dot(pick, s_ref[...]))
 
-    for half in range(halves):
+    def plane_dot(value, matrix, half, block):
+        cut = slice(2 * block * lanes, 2 * (block + 1) * lanes)
+        return dot3(value, (matrix[half, 0, :, cut], matrix[half, 1, :, cut]), ((1,), (0,)))
+
+    def arrive(half):
         pieces = [
             x_ref[:, h, half, ri].reshape(side * entries * rows, lanes) for ri in range(2) for h in range(2)
         ]
-        value = split_value(jnp.concatenate(pieces, axis=1))
-        d = dot3(value, (forward[half, 0], forward[half, 1]), ((1,), (0,)))
+        return split_value(jnp.concatenate(pieces, axis=1))
+
+    def to_plane(value, half, block):
+        d = plane_dot(value, forward, half, block)
         for ri in range(2):
-            mid[half, :, ri] = d[:, ri * plane : (ri + 1) * plane].reshape(side, entries, rows, plane)
-    for half in range(halves):
-        for e in range(entries):
-            for block in range(2):
-                cut = slice(block * lanes, (block + 1) * lanes)
-                values = [(mid[half, x, 0, e, :, cut], mid[half, x, 1, e, :, cut]) for x in range(side)]
-                for x, (re, im) in enumerate(dft_line(values, 1)):
-                    space[half, x, 0, e, :, cut] = re
-                    space[half, x, 1, e, :, cut] = im
+            piece = d[:, ri * lanes : (ri + 1) * lanes]
+            mid[half, block, ri] = piece.reshape(side, entries, rows, lanes)
+
+    def along_line(half, block, e):
+        values = [(mid[half, block, 0, x, e], mid[half, block, 1, x, e]) for x in range(side)]
+        for x, (re, im) in enumerate(dft_line(values, 1)):
+            space[half, block, x, 0, e] = re
+            space[half, block, x, 1, e] = im
+
+    def product(unit, block, c):
+        half, first = unit % halves, unit // halves * members
+        left, right = table_ref[first + c, 0], table_ref[first + c, 1]
+        values = []
+        for x in range(side):
+            other = mirror_ref[0, x]
+            a_re, a_im = space[half, block, x, 0, left], space[half, block, x, 1, left]
+            b_re, b_im = space[1 - half, block, other, 0, right], space[1 - half, block, other, 1, right]
+            values.append((a_re * b_re - a_im * b_im, a_re * b_im + a_im * b_re))
+        cut = slice(block * lanes, (block + 1) * lanes)
+        for x, (re, im) in enumerate(dft_line(values, -1)):
+            chi[unit, 0, x, c, :, cut] = re
+            chi[unit, 1, x, c, :, cut] = im
+
+    def from_plane(unit, value, h):
+        d = plane_dot(value, backward, unit % halves, h)
+        for ri in range(2):
+            piece = d[:, ri * lanes : (ri + 1) * lanes]
+            stage[unit, :, h, ri] = piece.reshape(side, members, rows, lanes)
+
+    def collect(unit):
+        count = side * members * rows
+        return split_value(jnp.concatenate([chi[unit, ri].reshape(count, plane) for ri in range(2)], axis=1))
 
     copies = []
-    for unit in range(units):
-        half, first = unit % halves, unit // halves * members
-        for c in range(members):
-            left, right = table_ref[first + c, 0], table_ref[first + c, 1]
-            for block in range(2):
-                cut = slice(block * lanes, (block + 1) * lanes)
-                values = []
-                for x in range(side):
-                    other = mirror_ref[0, x]
-                    a_re = space[half, x, 0, left, :, cut]
-                    a_im = space[half, x, 1, left, :, cut]
-                    b_re = space[1 - half, other, 0, right, :, cut]
-                    b_im = space[1 - half, other, 1, right, :, cut]
-                    values.append((a_re * b_re - a_im * b_im, a_re * b_im + a_im * b_re))
-                for x, (re, im) in enumerate(dft_line(values, -1)):
-                    chi[unit, 0, x, c, :, cut] = re
-                    chi[unit, 1, x, c, :, cut] = im
-        count = side * members * rows
-        value = jnp.concatenate([chi[unit, ri].reshape(count, plane) for ri in range(2)], axis=1)
-        d = dot3(split_value(value), (backward[half, 0], backward[half, 1]), ((1,), (0,)))
-        for ri in range(2):
-            for h in range(2):
-                start = ri * plane + h * lanes
-                stage[unit, :, h, ri] = d[:, start : start + lanes].reshape(side, members, rows, lanes)
-        target = out_ref.at[:, :, half, :, pl.ds(first, members)]
+
+    def send(unit):
+        target = out_ref.at[:, :, unit % halves, :, pl.ds(unit // halves * members, members)]
         copies.append(pltpu.make_async_copy(stage.at[unit], target, sems.at[unit]))
         copies[-1].start()
+
+    order = [(half, block) for half in range(halves) for block in range(2)]
+    for step in range(len(order) + 1):
+        if step < len(order):
+            half, block = order[step]
+            if block == 0:
+                value = arrive(half)
+            to_plane(value, half, block)
+        if step > 0:
+            for e in range(entries):
+                along_line(*order[step - 1], e)
+
+    for unit in range(units + 1):
+        tasks = [(block, c) for block in range(2) for c in range(members)] if unit < units else []
+        if unit > 0:
+            value = collect(unit - 1)
+        for h in range(2):
+            if unit > 0:
+                from_plane(unit - 1, value, h)
+            for block, c in tasks[h * members : (h + 1) * members]:
+                product(unit, block, c)
+        if unit > 0:
+            send(unit - 1)
     for copy in copies:
         copy.wait()
 
@@ -232,7 +294,6 @@
     smem = pl.BlockSpec(memory_space=pltpu.SMEM)
     vmem = pl.BlockSpec(memory_space=pltpu.VMEM)
     matrices = pltpu.VMEM((halves, 2, 2 * plane, 2 * plane), jnp.bfloat16)
-    spatial = pltpu.VMEM((halves, side, 2, entries, rows, plane), jnp.float32)
     return pl.pallas_call(
         middle_kernel,
         in_specs=[smem, smem] + [vmem] * 6,
@@ -241,8 +302,8 @@
         scratch_shapes=[
             matrices,
             matrices,
-            spatial,
-            spatial,
+            pltpu.VMEM((halves, 2, 2, side, entries, rows, lanes), jnp.float32),
+            pltpu.VMEM((halves, 2, side, 2, entries, rows, lanes), jnp.float32),
             pltpu.VMEM((units, 2, side, members, rows, plane), jnp.float32),
             pltpu.VMEM((units, side, 2, 2, members, rows, lanes), jnp.float32),
             pltpu.SemaphoreType.DMA((units,)),

time: 174 us -> 179 us (1.029)
  local copies, waits for them, and re-layouts: 0.2 us -> 5.19 us
    unnamed x17 -> x25, local copies, waits for them, and re-layouts: 0.12 us -> 5.11 us
where the time goes in v2:
time: 179 us
  blocking collectives  97.7 us (55%)
  waiting for transfers between devices  48.6 us (27%)
  Pallas kernels  19.7 us (11%)
  starting transfers between devices  7.3 us (4%)
  local copies, waits for them, and re-layouts  5.19 us (3%)
    all_to_all x1, blocking collectives, exchange(): lax.all_to_all(flat, 'kb', split_axis=0, concat_axis=0, tiled=True)  97.7 us
    all_to_all x1, waiting for transfers between devices, exchange(): lax.all_to_all(flat, 'kb', split_axis=0, concat_axis=0, tiled=True)  48.6 us
    pallas_call x1, Pallas kernels, middle(): pl.pallas_call(middle_kernel, in_specs=[smem, smem] + [vmem] * 6, out_spe...  10.5 us
    all_to_all x1, starting transfers between devices, exchange(): lax.all_to_all(flat, 'kb', split_axis=0, concat_axis=0, tiled=True)  7.3 us
    unnamed x25, local copies, waits for them, and re-layouts  5.11 us
    pallas_call x1, Pallas kernels, to_times(): pl.pallas_call(times_kernel, in_specs=[hbm] * 3, out_specs=hbm, out_shape...  4.7 us
    pallas_call x1, Pallas kernels, to_frequencies(): pl.pallas_call(frequency_kernel, in_specs=[vmem] * 3, out_specs=pl.BlockS...  4.53 us
  transfers between devices with their start and end apart: 1, of which 1 were waited for; matrix products, arithmetic and copies ran while one was open for 0% of the time, Pallas kernels for 0%

profile of v2, /device:TPU:0, one launch (start us, length us, event | category | flops | bytes accessed | tf_op | source)
XLA Modules:
  0.0 178.9 jit_solution(6481257562729733869)
XLA Ops:
  0.0 0.0 copy-start.1
  0.0 1.6 copy-done.1
  1.6 0.0 copy-start.4
  1.6 1.0 copy-done.4
  2.6 0.0 copy-start.5
  2.6 1.0 copy-done.5
  3.7 0.0 copy-start.11
  3.7 0.0 copy-start.10
  3.7 0.0 copy-start.6
  3.7 0.0 copy-start.8
  3.7 0.0 copy-start.9
  3.7 4.7 %to_times.1 = f32[32,2,2,4,8,128]{5,4,3,2,1,0:T(8,128)S(1)} custom-call(f32[2,4,128,512]{3,2,1,0:T(8,128)S(1)} %copy-done.1, bf16[512,512]{1,0:T(8,128)(2,1)S(1)} %copy-done.5, bf16[512,512]{1,0:T(8,128)(2,1)S(1)} %copy-done.4), custom_call_target="tpu_custom_call" | custom-call | tf_op jit(solution)/shard_map/to_times/pallas_call | solution.py:154
  8.4 0.0 copy-start
  8.4 1.3 copy-done
  9.7 7.3 %all-to-all-start = ((f32[32,128,128]{2,1,0:T(8,128)}), f32[32,128,128]{2,1,0:T(8,128)S(1)}, u32[]{:S(2)}, u32[]{:S(2)}) async-start(f32[32,128,128]{2,1,0:T(8,128)} %bitcast.10), calls=%async_computation | async-start | bytes 4194304 | tf_op jit(solution)/shard_map/all_to_all | solution.py:360
  17.0 0.0 copy-done.11
  17.1 0.1 copy.12.table_ref
  17.1 0.0 copy-done.10
  17.1 0.1 broadcast_add_fusion
  17.2 0.1 add.29.index_ref
  17.3 48.6 %all-to-all-done = f32[32,128,128]{2,1,0:T(8,128)S(1)} async-done(((f32[32,128,128]{2,1,0:T(8,128)}), f32[32,128,128]{2,1,0:T(8,128)S(1)}, u32[]{:S(2)}, u32[]{:S(2)}) %all-to-all-start) | async-done | bytes 2097184 | tf_op jit(solution)/shard_map/all_to_all | solution.py:360
  65.9 0.0 copy-done.6
  65.9 0.0 copy-done.7
  65.9 0.0 copy-done.8
  65.9 0.0 copy-done.9
  66.0 10.5 %middle.1 = f32[16,2,2,2,8,8,128]{6,5,4,3,2,1,0:T(8,128)} custom-call(s32[8,2]{1,0:T(8,128)S(1)} %copy.12.table_ref, s32[3,16]{1,0:T(4,128)S(1)} %copy-done.10, s32[1,256]{1,0:T(1,128)S(1)} %add.29.index_ref, f32[16,2,2,2,4,8,128]{6,5,4,3,2,1,0:T(8,128)S(1)} %bitcast.9, bf16[256,256]{1,0:T(8,128)(2,1)S(1)} %copy-done.9, bf16[256,256]{1,0:T(8,128)(2,1)S(1)} %copy-done.8, ...), custom_call_target="tpu_custom_call" | custom-call | tf_op jit(solution)/shard_map/middle/pallas_call | solution.py:297
  76.5 0.0 copy-start.2
  76.5 0.0 copy-start.3
  76.5 97.7 %all_to_all.10 = f32[32,256,128]{2,1,0:T(8,128)S(1)} all-to-all(f32[32,256,128]{2,1,0:T(8,128)} %bitcast.11), channel_id=1, replica_groups=mesh['set'=1,'kb'=32] {'kb'}, dimensions={0} | all-to-all | bytes 8388608 | tf_op jit(solution)/shard_map/all_to_all | solution.py:360
  174.2 0.0 copy-done.2
  174.2 0.0 copy-done.3
  174.2 4.5 %to_frequencies.1 = f32[2,8,128,512]{3,2,1,0:T(8,128)} custom-call(f32[32,2,2,8,8,128]{5,4,3,2,1,0:T(8,128)S(1)} %bitcast.8, bf16[512,512]{1,0:T(8,128)(2,1)S(1)} %copy-done.3, bf16[512,512]{1,0:T(8,128)(2,1)S(1)} %copy-done.2), custom_call_target="tpu_custom_call" | custom-call | tf_op jit(solution)/shard_map/to_frequencies/pallas_call | solution.py:346
  (2 shorter events, 0.0 us)
Async XLA Ops:
  0.0 1.6 copy-start.1
  1.6 1.0 copy-start.4
  2.6 1.0 copy-start.5
  3.7 13.4 %copy-start.11 = (s32[8,2]{0,1:T(2,128)S(1)}, s32[8,2]{0,1:T(2,128)}, u32[]{:S(2)}) copy-start(s32[8,2]{0,1:T(2,128)} %param.12) | copy-start | bytes 196
  3.7 13.5 %copy-start.10 = (s32[3,16]{1,0:T(4,128)S(1)}, s32[3,16]{1,0:T(4,128)}, u32[]{:S(2)}) copy-start(s32[3,16]{1,0:T(4,128)} %mirror_ref.1) | copy-start | bytes 580
  3.7 62.3 %copy-start.6 = (bf16[256,256]{1,0:T(8,128)(2,1)S(1)}, bf16[256,256]{1,0:T(8,128)(2,1)}, u32[]{:S(2)}) copy-start(bf16[256,256]{1,0:T(8,128)(2,1)} %constant.26.clone.sl_ref) | copy-start | bytes 393220
  3.7 62.3 %copy-start.7 = (bf16[256,256]{1,0:T(8,128)(2,1)S(1)}, bf16[256,256]{1,0:T(8,128)(2,1)}, u32[]{:S(2)}) copy-start(bf16[256,256]{1,0:T(8,128)(2,1)} %constant.25.clone.sh_ref) | copy-start | bytes 393220
  3.7 62.3 %copy-start.8 = (bf16[256,256]{1,0:T(8,128)(2,1)S(1)}, bf16[256,256]{1,0:T(8,128)(2,1)}, u32[]{:S(2)}) copy-start(bf16[256,256]{1,0:T(8,128)(2,1)} %constant.24.clone.cl_ref) | copy-start | bytes 393220
  3.7 62.3 %copy-start.9 = (bf16[256,256]{1,0:T(8,128)(2,1)S(1)}, bf16[256,256]{1,0:T(8,128)(2,1)}, u32[]{:S(2)}) copy-start(bf16[256,256]{1,0:T(8,128)(2,1)} %constant.23.clone.ch_ref) | copy-start | bytes 393220
  8.4 1.3 copy-start
  9.7 56.2 %all-to-all-start = ((f32[32,128,128]{2,1,0:T(8,128)}), f32[32,128,128]{2,1,0:T(8,128)S(1)}, u32[]{:S(2)}, u32[]{:S(2)}) async-start(f32[32,128,128]{2,1,0:T(8,128)} %bitcast.10), calls=%async_computation | async-start | bytes 4194304 | tf_op jit(solution)/shard_map/all_to_all | solution.py:360
  76.5 97.7 %copy-start.2 = (bf16[512,512]{1,0:T(8,128)(2,1)S(1)}, bf16[512,512]{1,0:T(8,128)(2,1)}, u32[]{:S(2)}) copy-start(bf16[512,512]{1,0:T(8,128)(2,1)} %constant.22.clone.ml_ref) | copy-start | bytes 1572868
  76.5 97.7 %copy-start.3 = (bf16[512,512]{1,0:T(8,128)(2,1)S(1)}, bf16[512,512]{1,0:T(8,128)(2,1)}, u32[]{:S(2)}) copy-start(bf16[512,512]{1,0:T(8,128)(2,1)} %constant.21.clone.mh_ref) | copy-start | bytes 1572868

commit v3 on v1

--- a/solution.py
+++ b/solution.py
@@ -152,9 +152,9 @@
 
 
 def middle_kernel(
-    table_ref, mirror_ref, index_ref, x_ref, ch_ref, cl_ref, sh_ref, sl_ref, out_ref,
-    forward, backward, mid, space, chi, stage, sems,
+    table_ref, mirror_ref, index_ref, me_ref, x_ref, ch_ref, cl_ref, sh_ref, sl_ref, *refs
 ):
+    outs, (forward, backward, mid, space, chi, stage, sems) = refs[:-7], refs[-7:]
     side, _, halves, _, entries, rows, lanes = x_ref.shape
     plane = 2 * lanes
     units, _, _, _, members, _, _ = stage.shape
@@ -213,9 +213,12 @@
             for h in range(2):
                 start = ri * plane + h * lanes
                 stage[unit, :, h, ri] = d[:, start : start + lanes].reshape(side, members, rows, lanes)
-        target = out_ref.at[:, :, half, :, pl.ds(first, members)]
-        copies.append(pltpu.make_async_copy(stage.at[unit], target, sems.at[unit]))
-        copies[-1].start()
+        for slot, out_ref in enumerate(outs):
+            target = me_ref[0] ^ slot
+            piece = stage.at[unit, target // 2, target % 2]
+            cut = out_ref.at[half, :, pl.ds(first, members)]
+            copies.append(pltpu.make_async_copy(piece, cut, sems.at[unit, slot]))
+            copies[-1].start()
     for copy in copies:
         copy.wait()
 
@@ -229,15 +232,18 @@
     index = (mirror_map[1][:, None] * side + mirror_map[2][None, :]).reshape(1, plane)
     cosine, sine = plane_parts(side)
     parts = [jnp.asarray(part) for part in split_constant(cosine) + split_constant(sine)]
+    devices = 2 * side
+    me = lax.axis_index("kb").astype(jnp.int32).reshape(1)
     smem = pl.BlockSpec(memory_space=pltpu.SMEM)
     vmem = pl.BlockSpec(memory_space=pltpu.VMEM)
+    hbm = pl.BlockSpec(memory_space=pltpu.HBM)
     matrices = pltpu.VMEM((halves, 2, 2 * plane, 2 * plane), jnp.bfloat16)
     spatial = pltpu.VMEM((halves, side, 2, entries, rows, plane), jnp.float32)
     return pl.pallas_call(
         middle_kernel,
-        in_specs=[smem, smem] + [vmem] * 6,
-        out_specs=pl.BlockSpec(memory_space=pltpu.HBM),
-        out_shape=jax.ShapeDtypeStruct((side, 2, halves, 2, components, rows, lanes), jnp.float32),
+        in_specs=[smem, smem, vmem, smem] + [vmem] * 5,
+        out_specs=[hbm] * devices,
+        out_shape=[jax.ShapeDtypeStruct((halves, 2, components, rows, lanes), jnp.float32)] * devices,
         scratch_shapes=[
             matrices,
             matrices,
@@ -245,14 +251,23 @@
             spatial,
             pltpu.VMEM((units, 2, side, members, rows, plane), jnp.float32),
             pltpu.VMEM((units, side, 2, 2, members, rows, lanes), jnp.float32),
-            pltpu.SemaphoreType.DMA((units,)),
+            pltpu.SemaphoreType.DMA((units, devices)),
         ],
         compiler_params=pltpu.CompilerParams(vmem_limit_bytes=48 << 20),
         name="middle",
-    )(table, mirror_map, index, x, *parts)
-
-
-def frequency_kernel(y_ref, mh_ref, ml_ref, out_ref, stage, sems):
+    )(table, mirror_map, index, me, x, *parts)
+
+
+def frequency_kernel(me_ref, mh_ref, ml_ref, *refs):
+    pieces, (out_ref, y_ref, stage, in_sems, sems) = refs[:-5], refs[-5:]
+    loads = [
+        pltpu.make_async_copy(piece, y_ref.at[me_ref[0] ^ slot], in_sems.at[slot])
+        for slot, piece in enumerate(pieces)
+    ]
+    for copy in loads:
+        copy.start()
+    for copy in loads:
+        copy.wait()
     devices, _, _, components, rows, lanes = y_ref.shape
     count = devices * rows
     groups = sems.shape[0]
@@ -278,25 +293,39 @@
         copy.wait()
 
 
-def to_frequencies(y, matrix):
-    components, lanes = y.shape[3], y.shape[5]
+def to_frequencies(pieces, matrix):
+    _, _, components, rows, lanes = pieces[0].shape
+    me = lax.axis_index("kb").astype(jnp.int32).reshape(1)
+    smem = pl.BlockSpec(memory_space=pltpu.SMEM)
+    hbm = pl.BlockSpec(memory_space=pltpu.HBM)
     shape = (2, components, lanes, matrix[0].shape[1])
     vmem = pl.BlockSpec(memory_space=pltpu.VMEM)
     return pl.pallas_call(
         frequency_kernel,
-        in_specs=[vmem] * 3,
-        out_specs=pl.BlockSpec(memory_space=pltpu.HBM),
+        in_specs=[smem, vmem, vmem] + [hbm] * len(pieces),
+        out_specs=hbm,
         out_shape=jax.ShapeDtypeStruct(shape, jnp.float32),
-        scratch_shapes=[pltpu.VMEM(shape, jnp.float32), pltpu.SemaphoreType.DMA((components // 2,))],
+        scratch_shapes=[
+            pltpu.VMEM((len(pieces),) + pieces[0].shape, jnp.float32),
+            pltpu.VMEM(shape, jnp.float32),
+            pltpu.SemaphoreType.DMA((len(pieces),)),
+            pltpu.SemaphoreType.DMA((components // 2,)),
+        ],
         compiler_params=pltpu.CompilerParams(vmem_limit_bytes=40 << 20),
         name="to_frequencies",
-    )(y, *matrix)
+    )(me, *matrix, *pieces)
 
 
 def exchange(x):
     shape = x.shape
     flat = x.reshape(shape[0], -1, shape[-1])
     return lax.all_to_all(flat, "kb", split_axis=0, concat_axis=0, tiled=True).reshape(shape)
+
+
+def swap(piece, slot, devices):
+    if slot == 0:
+        return piece
+    return lax.ppermute(piece, "kb", [(device, device ^ slot) for device in range(devices)])
 
 
 def local(green, pair_table, mirror_map):
@@ -318,15 +347,22 @@
         x = jnp.moveaxis(x, 2, -2)
         return x.reshape(x.shape[:-2] + (strips * lanes,))
 
-    def returned(x):
-        x = x[..., :pairs, :]
+    def returned(pieces):
+        if lanes == LANES and pairs == padded:
+            half = devices // 2
+            order = [slot for near in range(half) for slot in (near + half, near)]
+            moved = {slot: swap(pieces[slot], slot, devices) for slot in order}
+            return [moved[slot] for slot in range(devices)]
+        x = jnp.stack(pieces)[lax.axis_index("kb") ^ jnp.arange(2 * side)]
+        x = x.reshape((side, 2) + x.shape[1:])[..., :pairs, :]
         x = x.reshape(x.shape[:-1] + (strips, lanes))
         x = jnp.moveaxis(x, -2, 2)
         x = exchange(x.reshape((devices,) + x.shape[3:]))
-        return jnp.pad(x, ((0, 0),) * 4 + ((0, padded - pairs), (0, 0)))
-
-    chi = middle(arrived(to_times(green, devices, padded, forward)), pair_table, mirror_map)
-    return to_frequencies(returned(chi), backward)
+        x = jnp.pad(x, ((0, 0),) * 4 + ((0, padded - pairs), (0, 0)))
+        return list(x[lax.axis_index("kb") ^ jnp.arange(devices)])
+
+    pieces = middle(arrived(to_times(green, devices, padded, forward)), pair_table, mirror_map)
+    return to_frequencies(returned(pieces), backward)
 
 
 def solution(mesh):

time: 174 us -> 209 us (1.20)
  the two profiles are of different devices: /device:TPU:0 before, /device:TPU:9 now
where the time goes in v3:
time: 209 us; the launch traced here: 208 us
  waiting for transfers between devices  115 us (55%)
  starting transfers between devices  60.2 us (29%)
  Pallas kernels  32.1 us (15%)
    ppermute x31, waiting for transfers between devices, swap(): lax.ppermute(piece, 'kb', [(device, device ^ slot) for device in range(de...  68.4 us
    ppermute x31, starting transfers between devices, swap(): lax.ppermute(piece, 'kb', [(device, device ^ slot) for device in range(de...  53.8 us
    all_to_all x1, waiting for transfers between devices, exchange(): lax.all_to_all(flat, 'kb', split_axis=0, concat_axis=0, tiled=True)  46.9 us
    pallas_call x1, Pallas kernels, middle(): pl.pallas_call(middle_kernel, in_specs=[smem, smem, vmem, smem] + [vmem]...  15.7 us
    pallas_call x1, Pallas kernels, to_frequencies(): pl.pallas_call(frequency_kernel, in_specs=[smem, vmem, vmem] + [hbm] * le...  11.2 us
    all_to_all x1, starting transfers between devices, exchange(): lax.all_to_all(flat, 'kb', split_axis=0, concat_axis=0, tiled=True)  6.42 us
    pallas_call x1, Pallas kernels, to_times(): pl.pallas_call(times_kernel, grid=(entries,), in_specs=[pl.BlockSpec((2,...  5.29 us
  transfers between devices with their start and end apart: 32, of which 18 were waited for; matrix products, arithmetic and copies ran while one was open for 0% of the time, Pallas kernels for 0%

profile of v3, /device:TPU:9, one launch (start us, length us, event | category | flops | bytes accessed | tf_op | source)
XLA Modules:
  0.0 208.3 jit_solution(15511624874406223251)
XLA Ops:
  0.0 5.3 %to_times.1 = f32[32,2,2,4,8,128]{5,4,3,2,1,0:T(8,128)} custom-call(f32[2,4,128,512]{3,2,1,0:T(8,128)} %g_ref.1, bf16[512,512]{1,0:T(8,128)(2,1)} %constant.9.clone.mh_ref, bf16[512,512]{1,0:T(8,128)(2,1)} %constant.24.clone.ml_ref), custom_call_target="tpu_custom_call" | custom-call | tf_op jit(solution)/shard_map/to_times/pallas_call | solution.py:131
  5.3 6.4 %all-to-all-start = ((f32[32,128,128]{2,1,0:T(8,128)}), f32[32,128,128]{2,1,0:T(8,128)}, u32[]{:S(2)}, u32[]{:S(2)}) async-start(f32[32,128,128]{2,1,0:T(8,128)} %bitcast.7), calls=%async_computation | async-start | bytes 4194304 | tf_op jit(solution)/shard_map/all_to_all | solution.py:322
  12.1 46.9 %all-to-all-done = f32[32,128,128]{2,1,0:T(8,128)} async-done(((f32[32,128,128]{2,1,0:T(8,128)}), f32[32,128,128]{2,1,0:T(8,128)}, u32[]{:S(2)}, u32[]{:S(2)}) %all-to-all-start) | async-done | bytes 2097184 | tf_op jit(solution)/shard_map/all_to_all | solution.py:322
  59.0 15.7 %middle.1 = (f32[2,2,8,8,128]{4,3,2,1,0:T(8,128)S(1)}, f32[2,2,8,8,128]{4,3,2,1,0:T(8,128)S(1)}, f32[2,2,8,8,128]{4,3,2,1,0:T(8,128)S(1)}, f32[2,2,8,8,128]{4,3,...) custom-call(s32[8,2]{1,0:T(8,128)S(1)} %copy.12.table_ref, ...), custom_call_target="tpu_custom_call" | custom-call | tf_op jit(solution)/shard_map/middle/pallas_call | solution.py:242
  79.7 2.7 %collective-permute-start.6 = (f32[2,2,8,8,128]{4,3,2,1,0:T(8,128)S(1)}, f32[2,2,8,8,128]{4,3,2,1,0:T(8,128)S(1)}, u32[]{:S(2)}, u32[]{:S(2)}) collective-permute-start(f32[2,2,8,8,128]{4,3,2,1,0:T(8,128)S(1)} %get-tuple-element.44), channel_id=1, source_target_pairs={{0,7},{1,6},{2,5},{3,4},{4,3},{5,2},{6,1},{7,0},{8,15},{9,14},{10,... | collective-permute-start | bytes 393224 | tf_op jit(solution)/shard_map/ppermute | solution.py:328
  84.0 1.6 collective-permute-start.7
  85.6 5.2 %collective-permute-done.4.refs_5_ = f32[2,2,8,8,128]{4,3,2,1,0:T(8,128)S(1)} collective-permute-done((f32[2,2,8,8,128]{4,3,2,1,0:T(8,128)S(1)}, f32[2,2,8,8,128]{4,3,2,1,0:T(8,128)S(1)}, u32[]{:S(2)}, u32[]{:S(2)}) %collective-permute-start.4) | collective-permute-done | bytes 131104 | tf_op jit(solution)/shard_map/ppermute | solution.py:328
  90.8 2.5 %collective-permute-start.9 = (f32[2,2,8,8,128]{4,3,2,1,0:T(8,128)S(1)}, f32[2,2,8,8,128]{4,3,2,1,0:T(8,128)S(1)}, u32[]{:S(2)}, u32[]{:S(2)}) collective-permute-start(f32[2,2,8,8,128]{4,3,2,1,0:T(8,128)S(1)} %get-tuple-element.47), channel_id=1, source_target_pairs={{0,10},{1,11},{2,8},{3,9},{4,14},{5,15},{6,12},{7,13},{8,2},{9,3},... | collective-permute-start | bytes 393224 | tf_op jit(solution)/shard_map/ppermute | solution.py:328
  93.4 2.1 %collective-permute-start.11 = (f32[2,2,8,8,128]{4,3,2,1,0:T(8,128)S(1)}, f32[2,2,8,8,128]{4,3,2,1,0:T(8,128)S(1)}, u32[]{:S(2)}, u32[]{:S(2)}) collective-permute-start(f32[2,2,8,8,128]{4,3,2,1,0:T(8,128)S(1)} %get-tuple-element.49), channel_id=1, source_target_pairs={{0,12},{1,13},{2,14},{3,15},{4,8},{5,9},{6,10},{7,11},{8,4},{9,5},... | collective-permute-start | bytes 393224 | tf_op jit(solution)/shard_map/ppermute | solution.py:328
  96.3 3.2 %collective-permute-start.13 = (f32[2,2,8,8,128]{4,3,2,1,0:T(8,128)S(1)}, f32[2,2,8,8,128]{4,3,2,1,0:T(8,128)S(1)}, u32[]{:S(2)}, u32[]{:S(2)}) collective-permute-start(f32[2,2,8,8,128]{4,3,2,1,0:T(8,128)S(1)} %get-tuple-element.51), channel_id=1, source_target_pairs={{0,14},{1,15},{2,12},{3,13},{4,10},{5,11},{6,8},{7,9},{8,6},{9,7},... | collective-permute-start | bytes 393224 | tf_op jit(solution)/shard_map/ppermute | solution.py:328
  99.5 1.6 collective-permute-start.14
  102.7 3.7 %collective-permute-start.16 = (f32[2,2,8,8,128]{4,3,2,1,0:T(8,128)S(1)}, f32[2,2,8,8,128]{4,3,2,1,0:T(8,128)S(1)}, u32[]{:S(2)}, u32[]{:S(2)}) collective-permute-start(f32[2,2,8,8,128]{4,3,2,1,0:T(8,128)S(1)} %get-tuple-element.54), channel_id=1, source_target_pairs={{0,17},{1,16},{2,19},{3,18},{4,21},{5,20},{6,23},{7,22},{8,25},{9,... | collective-permute-start | bytes 393224 | tf_op jit(solution)/shard_map/ppermute | solution.py:328
  106.4 3.9 %collective-permute-done.12.refs_13_ = f32[2,2,8,8,128]{4,3,2,1,0:T(8,128)S(1)} collective-permute-done((f32[2,2,8,8,128]{4,3,2,1,0:T(8,128)S(1)}, f32[2,2,8,8,128]{4,3,2,1,0:T(8,128)S(1)}, u32[]{:S(2)}, u32[]{:S(2)}) %collective-permute-start.12) | collective-permute-done | bytes 131104 | tf_op jit(solution)/shard_map/ppermute | solution.py:328
  110.3 3.4 %collective-permute-start.17 = (f32[2,2,8,8,128]{4,3,2,1,0:T(8,128)S(1)}, f32[2,2,8,8,128]{4,3,2,1,0:T(8,128)S(1)}, u32[]{:S(2)}, u32[]{:S(2)}) collective-permute-start(f32[2,2,8,8,128]{4,3,2,1,0:T(8,128)S(1)} %get-tuple-element.55), channel_id=1, source_target_pairs={{0,18},{1,19},{2,16},{3,17},{4,22},{5,23},{6,20},{7,21},{8,26},{9,... | collective-permute-start | bytes 393224 | tf_op jit(solution)/shard_map/ppermute | solution.py:328
  113.7 4.8 %collective-permute-start.18 = (f32[2,2,8,8,128]{4,3,2,1,0:T(8,128)S(1)}, f32[2,2,8,8,128]{4,3,2,1,0:T(8,128)S(1)}, u32[]{:S(2)}, u32[]{:S(2)}) collective-permute-start(f32[2,2,8,8,128]{4,3,2,1,0:T(8,128)S(1)} %get-tuple-element.56), channel_id=1, source_target_pairs={{0,19},{1,18},{2,17},{3,16},{4,23},{5,22},{6,21},{7,20},{8,27},{9,... | collective-permute-start | bytes 393224 | tf_op jit(solution)/shard_map/ppermute | solution.py:328
  119.8 1.7 collective-permute-start.20
  121.5 2.5 %collective-permute-start.21 = (f32[2,2,8,8,128]{4,3,2,1,0:T(8,128)S(1)}, f32[2,2,8,8,128]{4,3,2,1,0:T(8,128)S(1)}, u32[]{:S(2)}, u32[]{:S(2)}) collective-permute-start(f32[2,2,8,8,128]{4,3,2,1,0:T(8,128)S(1)} %get-tuple-element.59), channel_id=1, source_target_pairs={{0,22},{1,23},{2,20},{3,21},{4,18},{5,19},{6,16},{7,17},{8,30},{9,... | collective-permute-start | bytes 393224 | tf_op jit(solution)/shard_map/ppermute | solution.py:328
  124.0 8.8 %collective-permute-done.17.refs_18_ = f32[2,2,8,8,128]{4,3,2,1,0:T(8,128)S(1)} collective-permute-done((f32[2,2,8,8,128]{4,3,2,1,0:T(8,128)S(1)}, f32[2,2,8,8,128]{4,3,2,1,0:T(8,128)S(1)}, u32[]{:S(2)}, u32[]{:S(2)}) %collective-permute-start.17) | collective-permute-done | bytes 131104 | tf_op jit(solution)/shard_map/ppermute | solution.py:328
  132.7 4.4 %collective-permute-start.22 = (f32[2,2,8,8,128]{4,3,2,1,0:T(8,128)S(1)}, f32[2,2,8,8,128]{4,3,2,1,0:T(8,128)S(1)}, u32[]{:S(2)}, u32[]{:S(2)}) collective-permute-start(f32[2,2,8,8,128]{4,3,2,1,0:T(8,128)S(1)} %get-tuple-element.60), channel_id=1, source_target_pairs={{0,23},{1,22},{2,21},{3,20},{4,19},{5,18},{6,17},{7,16},{8,31},{9,... | collective-permute-start | bytes 393224 | tf_op jit(solution)/shard_map/ppermute | solution.py:328
  137.8 6.1 %collective-permute-done.19.refs_20_ = f32[2,2,8,8,128]{4,3,2,1,0:T(8,128)S(1)} collective-permute-done((f32[2,2,8,8,128]{4,3,2,1,0:T(8,128)S(1)}, f32[2,2,8,8,128]{4,3,2,1,0:T(8,128)S(1)}, u32[]{:S(2)}, u32[]{:S(2)}) %collective-permute-start.19) | collective-permute-done | bytes 131104 | tf_op jit(solution)/shard_map/ppermute | solution.py:328
  144.9 1.9 collective-permute-done.20.refs_21_
  148.1 4.1 %collective-permute-done.21.refs_22_ = f32[2,2,8,8,128]{4,3,2,1,0:T(8,128)S(1)} collective-permute-done((f32[2,2,8,8,128]{4,3,2,1,0:T(8,128)S(1)}, f32[2,2,8,8,128]{4,3,2,1,0:T(8,128)S(1)}, u32[]{:S(2)}, u32[]{:S(2)}) %collective-permute-start.21) | collective-permute-done | bytes 131104 | tf_op jit(solution)/shard_map/ppermute | solution.py:328
  152.2 4.6 %collective-permute-start.26 = (f32[2,2,8,8,128]{4,3,2,1,0:T(8,128)S(1)}, f32[2,2,8,8,128]{4,3,2,1,0:T(8,128)S(1)}, u32[]{:S(2)}, u32[]{:S(2)}) collective-permute-start(f32[2,2,8,8,128]{4,3,2,1,0:T(8,128)S(1)} %get-tuple-element.64), channel_id=1, source_target_pairs={{0,27},{1,26},{2,25},{3,24},{4,31},{5,30},{6,29},{7,28},{8,19},{9,... | collective-permute-start | bytes 393224 | tf_op jit(solution)/shard_map/ppermute | solution.py:328
  158.7 6.2 %collective-permute-done.23.refs_24_ = f32[2,2,8,8,128]{4,3,2,1,0:T(8,128)S(1)} collective-permute-done((f32[2,2,8,8,128]{4,3,2,1,0:T(8,128)S(1)}, f32[2,2,8,8,128]{4,3,2,1,0:T(8,128)S(1)}, u32[]{:S(2)}, u32[]{:S(2)}) %collective-permute-start.23) | collective-permute-done | bytes 131104 | tf_op jit(solution)/shard_map/ppermute | solution.py:328
  164.9 14.0 %collective-permute-done.24.refs_25_ = f32[2,2,8,8,128]{4,3,2,1,0:T(8,128)S(1)} collective-permute-done((f32[2,2,8,8,128]{4,3,2,1,0:T(8,128)S(1)}, f32[2,2,8,8,128]{4,3,2,1,0:T(8,128)S(1)}, u32[]{:S(2)}, u32[]{:S(2)}) %collective-permute-start.24) | collective-permute-done | bytes 131104 | tf_op jit(solution)/shard_map/ppermute | solution.py:328
  179.0 1.8 collective-permute-start.29
  180.8 1.8 collective-permute-done.25.refs_26_
  185.4 2.2 %collective-permute-done.27.refs_28_ = f32[2,2,8,8,128]{4,3,2,1,0:T(8,128)S(1)} collective-permute-done((f32[2,2,8,8,128]{4,3,2,1,0:T(8,128)S(1)}, f32[2,2,8,8,128]{4,3,2,1,0:T(8,128)S(1)}, u32[]{:S(2)}, u32[]{:S(2)}) %collective-permute-start.27) | collective-permute-done | bytes 131104 | tf_op jit(solution)/shard_map/ppermute | solution.py:328
  187.5 2.8 %collective-permute-done.28.refs_29_ = f32[2,2,8,8,128]{4,3,2,1,0:T(8,128)S(1)} collective-permute-done((f32[2,2,8,8,128]{4,3,2,1,0:T(8,128)S(1)}, f32[2,2,8,8,128]{4,3,2,1,0:T(8,128)S(1)}, u32[]{:S(2)}, u32[]{:S(2)}) %collective-permute-start.28) | collective-permute-done | bytes 131104 | tf_op jit(solution)/shard_map/ppermute | solution.py:328
  190.4 3.8 %collective-permute-done.29.refs_30_ = f32[2,2,8,8,128]{4,3,2,1,0:T(8,128)S(1)} collective-permute-done((f32[2,2,8,8,128]{4,3,2,1,0:T(8,128)S(1)}, f32[2,2,8,8,128]{4,3,2,1,0:T(8,128)S(1)}, u32[]{:S(2)}, u32[]{:S(2)}) %collective-permute-start.29) | collective-permute-done | bytes 131104 | tf_op jit(solution)/shard_map/ppermute | solution.py:328
  194.2 2.8 %collective-permute-done.30.refs_31_ = f32[2,2,8,8,128]{4,3,2,1,0:T(8,128)S(1)} collective-permute-done((f32[2,2,8,8,128]{4,3,2,1,0:T(8,128)S(1)}, f32[2,2,8,8,128]{4,3,2,1,0:T(8,128)S(1)}, u32[]{:S(2)}, u32[]{:S(2)}) %collective-permute-start.30) | collective-permute-done | bytes 131104 | tf_op jit(solution)/shard_map/ppermute | solution.py:328
  197.0 11.2 %to_frequencies.1 = f32[2,8,128,512]{3,2,1,0:T(8,128)} custom-call(s32[1]{0:T(128)} %bitcast.me_ref, bf16[512,512]{1,0:T(8,128)(2,1)S(1)} %copy-done.1, bf16[512,512]{1,0:T(8,128)(2,1)S(1)} %copy-done, f32[2,2,8,8,128]{4,3,2,1,0:T(8,128)S(1)} %get-tuple-element.37.refs_0_, f32[2,2,8,8,128]{4,3,2,1,0:T(8,128)S(1)} %collective-permute-done.refs_1_, ...), custom_call_target="tpu_custom_call" | custom-call | tf_op jit(solution)/shard_map/to_frequencies/pallas_call | solution.py:303
  (55 shorter events, 18.3 us)
Async XLA Ops:
  5.3 53.6 %all-to-all-start = ((f32[32,128,128]{2,1,0:T(8,128)}), f32[32,128,128]{2,1,0:T(8,128)}, u32[]{:S(2)}, u32[]{:S(2)}) async-start(f32[32,128,128]{2,1,0:T(8,128)} %bitcast.7), calls=%async_computation | async-start | bytes 4194304 | tf_op jit(solution)/shard_map/all_to_all | solution.py:322
  74.7 3.7 %collective-permute-start = (f32[2,2,8,8,128]{4,3,2,1,0:T(8,128)S(1)}, f32[2,2,8,8,128]{4,3,2,1,0:T(8,128)S(1)}, u32[]{:S(2)}, u32[]{:S(2)}) collective-permute-start(f32[2,2,8,8,128]{4,3,2,1,0:T(8,128)S(1)} %get-tuple-element.38), channel_id=1, source_target_pairs={{0,1},{1,0},{2,3},{3,2},{4,5},{5,4},{6,7},{7,6},{8,9},{9,8},{10,11... | collective-permute-start | bytes 393224 | tf_op jit(solution)/shard_map/ppermute | solution.py:328
  74.8 4.9 %collective-permute-start.1 = (f32[2,2,8,8,128]{4,3,2,1,0:T(8,128)S(1)}, f32[2,2,8,8,128]{4,3,2,1,0:T(8,128)S(1)}, u32[]{:S(2)}, u32[]{:S(2)}) collective-permute-start(f32[2,2,8,8,128]{4,3,2,1,0:T(8,128)S(1)} %get-tuple-element.39), channel_id=1, source_target_pairs={{0,2},{1,3},{2,0},{3,1},{4,6},{5,7},{6,4},{7,5},{8,10},{9,11},{10,... | collective-permute-start | bytes 393224 | tf_op jit(solution)/shard_map/ppermute | solution.py:328
  76.1 8.0 %collective-permute-start.2 = (f32[2,2,8,8,128]{4,3,2,1,0:T(8,128)S(1)}, f32[2,2,8,8,128]{4,3,2,1,0:T(8,128)S(1)}, u32[]{:S(2)}, u32[]{:S(2)}) collective-permute-start(f32[2,2,8,8,128]{4,3,2,1,0:T(8,128)S(1)} %get-tuple-element.40), channel_id=1, source_target_pairs={{0,3},{1,2},{2,1},{3,0},{4,7},{5,6},{6,5},{7,4},{8,11},{9,10},{10,... | collective-permute-start | bytes 393224 | tf_op jit(solution)/shard_map/ppermute | solution.py:328
  76.9 8.7 %collective-permute-start.3 = (f32[2,2,8,8,128]{4,3,2,1,0:T(8,128)S(1)}, f32[2,2,8,8,128]{4,3,2,1,0:T(8,128)S(1)}, u32[]{:S(2)}, u32[]{:S(2)}) collective-permute-start(f32[2,2,8,8,128]{4,3,2,1,0:T(8,128)S(1)} %get-tuple-element.41), channel_id=1, source_target_pairs={{0,4},{1,5},{2,6},{3,7},{4,0},{5,1},{6,2},{7,3},{8,12},{9,13},{10,... | collective-permute-start | bytes 393224 | tf_op jit(solution)/shard_map/ppermute | solution.py:328
  77.4 13.4 %collective-permute-start.4 = (f32[2,2,8,8,128]{4,3,2,1,0:T(8,128)S(1)}, f32[2,2,8,8,128]{4,3,2,1,0:T(8,128)S(1)}, u32[]{:S(2)}, u32[]{:S(2)}) collective-permute-start(f32[2,2,8,8,128]{4,3,2,1,0:T(8,128)S(1)} %get-tuple-element.42), channel_id=1, source_target_pairs={{0,5},{1,4},{2,7},{3,6},{4,1},{5,0},{6,3},{7,2},{8,13},{9,12},{10,... | collective-permute-start | bytes 393224 | tf_op jit(solution)/shard_map/ppermute | solution.py:328
  78.4 14.9 %collective-permute-start.5 = (f32[2,2,8,8,128]{4,3,2,1,0:T(8,128)S(1)}, f32[2,2,8,8,128]{4,3,2,1,0:T(8,128)S(1)}, u32[]{:S(2)}, u32[]{:S(2)}) collective-permute-start(f32[2,2,8,8,128]{4,3,2,1,0:T(8,128)S(1)} %get-tuple-element.43), channel_id=1, source_target_pairs={{0,6},{1,7},{2,4},{3,5},{4,2},{5,3},{6,0},{7,1},{8,14},{9,15},{10,... | collective-permute-start | bytes 393224 | tf_op jit(solution)/shard_map/ppermute | solution.py:328
  79.7 13.7 %collective-permute-start.6 = (f32[2,2,8,8,128]{4,3,2,1,0:T(8,128)S(1)}, f32[2,2,8,8,128]{4,3,2,1,0:T(8,128)S(1)}, u32[]{:S(2)}, u32[]{:S(2)}) collective-permute-start(f32[2,2,8,8,128]{4,3,2,1,0:T(8,128)S(1)} %get-tuple-element.44), channel_id=1, source_target_pairs={{0,7},{1,6},{2,5},{3,4},{4,3},{5,2},{6,1},{7,0},{8,15},{9,14},{10,... | collective-permute-start | bytes 393224 | tf_op jit(solution)/shard_map/ppermute | solution.py:328
  84.0 11.5 %collective-permute-start.7 = (f32[2,2,8,8,128]{4,3,2,1,0:T(8,128)S(1)}, f32[2,2,8,8,128]{4,3,2,1,0:T(8,128)S(1)}, u32[]{:S(2)}, u32[]{:S(2)}) collective-permute-start(f32[2,2,8,8,128]{4,3,2,1,0:T(8,128)S(1)} %get-tuple-element.45), channel_id=1, source_target_pairs={{0,8},{1,9},{2,10},{3,11},{4,12},{5,13},{6,14},{7,15},{8,0},{9,1},... | collective-permute-start | bytes 393224 | tf_op jit(solution)/shard_map/ppermute | solution.py:328
  85.6 10.7 %collective-permute-start.8 = (f32[2,2,8,8,128]{4,3,2,1,0:T(8,128)S(1)}, f32[2,2,8,8,128]{4,3,2,1,0:T(8,128)S(1)}, u32[]{:S(2)}, u32[]{:S(2)}) collective-permute-start(f32[2,2,8,8,128]{4,3,2,1,0:T(8,128)S(1)} %get-tuple-element.46), channel_id=1, source_target_pairs={{0,9},{1,8},{2,11},{3,10},{4,13},{5,12},{6,15},{7,14},{8,1},{9,0},... | collective-permute-start | bytes 393224 | tf_op jit(solution)/shard_map/ppermute | solution.py:328
  90.8 8.6 %collective-permute-start.9 = (f32[2,2,8,8,128]{4,3,2,1,0:T(8,128)S(1)}, f32[2,2,8,8,128]{4,3,2,1,0:T(8,128)S(1)}, u32[]{:S(2)}, u32[]{:S(2)}) collective-permute-start(f32[2,2,8,8,128]{4,3,2,1,0:T(8,128)S(1)} %get-tuple-element.47), channel_id=1, source_target_pairs={{0,10},{1,11},{2,8},{3,9},{4,14},{5,15},{6,12},{7,13},{8,2},{9,3},... | collective-permute-start | bytes 393224 | tf_op jit(solution)/shard_map/ppermute | solution.py:328
  93.3 7.8 %collective-permute-start.10 = (f32[2,2,8,8,128]{4,3,2,1,0:T(8,128)S(1)}, f32[2,2,8,8,128]{4,3,2,1,0:T(8,128)S(1)}, u32[]{:S(2)}, u32[]{:S(2)}) collective-permute-start(f32[2,2,8,8,128]{4,3,2,1,0:T(8,128)S(1)} %get-tuple-element.48), channel_id=1, source_target_pairs={{0,11},{1,10},{2,9},{3,8},{4,15},{5,14},{6,13},{7,12},{8,3},{9,2},... | collective-permute-start | bytes 393224 | tf_op jit(solution)/shard_map/ppermute | solution.py:328
  93.4 9.2 %collective-permute-start.11 = (f32[2,2,8,8,128]{4,3,2,1,0:T(8,128)S(1)}, f32[2,2,8,8,128]{4,3,2,1,0:T(8,128)S(1)}, u32[]{:S(2)}, u32[]{:S(2)}) collective-permute-start(f32[2,2,8,8,128]{4,3,2,1,0:T(8,128)S(1)} %get-tuple-element.49), channel_id=1, source_target_pairs={{0,12},{1,13},{2,14},{3,15},{4,8},{5,9},{6,10},{7,11},{8,4},{9,5},... | collective-permute-start | bytes 393224 | tf_op jit(solution)/shard_map/ppermute | solution.py:328
  95.6 14.7 %collective-permute-start.12 = (f32[2,2,8,8,128]{4,3,2,1,0:T(8,128)S(1)}, f32[2,2,8,8,128]{4,3,2,1,0:T(8,128)S(1)}, u32[]{:S(2)}, u32[]{:S(2)}) collective-permute-start(f32[2,2,8,8,128]{4,3,2,1,0:T(8,128)S(1)} %get-tuple-element.50), channel_id=1, source_target_pairs={{0,13},{1,12},{2,15},{3,14},{4,9},{5,8},{6,11},{7,10},{8,5},{9,4},... | collective-permute-start | bytes 393224 | tf_op jit(solution)/shard_map/ppermute | solution.py:328
  96.3 17.4 %collective-permute-start.13 = (f32[2,2,8,8,128]{4,3,2,1,0:T(8,128)S(1)}, f32[2,2,8,8,128]{4,3,2,1,0:T(8,128)S(1)}, u32[]{:S(2)}, u32[]{:S(2)}) collective-permute-start(f32[2,2,8,8,128]{4,3,2,1,0:T(8,128)S(1)} %get-tuple-element.51), channel_id=1, source_target_pairs={{0,14},{1,15},{2,12},{3,13},{4,10},{5,11},{6,8},{7,9},{8,6},{9,7},... | collective-permute-start | bytes 393224 | tf_op jit(solution)/shard_map/ppermute | solution.py:328
  99.5 19.0 %collective-permute-start.14 = (f32[2,2,8,8,128]{4,3,2,1,0:T(8,128)S(1)}, f32[2,2,8,8,128]{4,3,2,1,0:T(8,128)S(1)}, u32[]{:S(2)}, u32[]{:S(2)}) collective-permute-start(f32[2,2,8,8,128]{4,3,2,1,0:T(8,128)S(1)} %get-tuple-element.52), channel_id=1, source_target_pairs={{0,15},{1,14},{2,13},{3,12},{4,11},{5,10},{6,9},{7,8},{8,7},{9,6},... | collective-permute-start | bytes 393224 | tf_op jit(solution)/shard_map/ppermute | solution.py:328
  101.1 18.7 %collective-permute-start.15 = (f32[2,2,8,8,128]{4,3,2,1,0:T(8,128)S(1)}, f32[2,2,8,8,128]{4,3,2,1,0:T(8,128)S(1)}, u32[]{:S(2)}, u32[]{:S(2)}) collective-permute-start(f32[2,2,8,8,128]{4,3,2,1,0:T(8,128)S(1)} %get-tuple-element.53), channel_id=1, source_target_pairs={{0,16},{1,17},{2,18},{3,19},{4,20},{5,21},{6,22},{7,23},{8,24},{9,... | collective-permute-start | bytes 393224 | tf_op jit(solution)/shard_map/ppermute | solution.py:328
  102.7 18.8 %collective-permute-start.16 = (f32[2,2,8,8,128]{4,3,2,1,0:T(8,128)S(1)}, f32[2,2,8,8,128]{4,3,2,1,0:T(8,128)S(1)}, u32[]{:S(2)}, u32[]{:S(2)}) collective-permute-start(f32[2,2,8,8,128]{4,3,2,1,0:T(8,128)S(1)} %get-tuple-element.54), channel_id=1, source_target_pairs={{0,17},{1,16},{2,19},{3,18},{4,21},{5,20},{6,23},{7,22},{8,25},{9,... | collective-permute-start | bytes 393224 | tf_op jit(solution)/shard_map/ppermute | solution.py:328
  110.3 22.4 %collective-permute-start.17 = (f32[2,2,8,8,128]{4,3,2,1,0:T(8,128)S(1)}, f32[2,2,8,8,128]{4,3,2,1,0:T(8,128)S(1)}, u32[]{:S(2)}, u32[]{:S(2)}) collective-permute-start(f32[2,2,8,8,128]{4,3,2,1,0:T(8,128)S(1)} %get-tuple-element.55), channel_id=1, source_target_pairs={{0,18},{1,19},{2,16},{3,17},{4,22},{5,23},{6,20},{7,21},{8,26},{9,... | collective-permute-start | bytes 393224 | tf_op jit(solution)/shard_map/ppermute | solution.py:328
  113.7 23.4 %collective-permute-start.18 = (f32[2,2,8,8,128]{4,3,2,1,0:T(8,128)S(1)}, f32[2,2,8,8,128]{4,3,2,1,0:T(8,128)S(1)}, u32[]{:S(2)}, u32[]{:S(2)}) collective-permute-start(f32[2,2,8,8,128]{4,3,2,1,0:T(8,128)S(1)} %get-tuple-element.56), channel_id=1, source_target_pairs={{0,19},{1,18},{2,17},{3,16},{4,23},{5,22},{6,21},{7,20},{8,27},{9,... | collective-permute-start | bytes 393224 | tf_op jit(solution)/shard_map/ppermute | solution.py:328
  118.5 25.5 %collective-permute-start.19 = (f32[2,2,8,8,128]{4,3,2,1,0:T(8,128)S(1)}, f32[2,2,8,8,128]{4,3,2,1,0:T(8,128)S(1)}, u32[]{:S(2)}, u32[]{:S(2)}) collective-permute-start(f32[2,2,8,8,128]{4,3,2,1,0:T(8,128)S(1)} %get-tuple-element.57), channel_id=1, source_target_pairs={{0,20},{1,21},{2,22},{3,23},{4,16},{5,17},{6,18},{7,19},{8,28},{9,... | collective-permute-start | bytes 393224 | tf_op jit(solution)/shard_map/ppermute | solution.py:328
  119.8 27.0 %collective-permute-start.20 = (f32[2,2,8,8,128]{4,3,2,1,0:T(8,128)S(1)}, f32[2,2,8,8,128]{4,3,2,1,0:T(8,128)S(1)}, u32[]{:S(2)}, u32[]{:S(2)}) collective-permute-start(f32[2,2,8,8,128]{4,3,2,1,0:T(8,128)S(1)} %get-tuple-element.58), channel_id=1, source_target_pairs={{0,21},{1,20},{2,23},{3,22},{4,17},{5,16},{6,19},{7,18},{8,29},{9,... | collective-permute-start | bytes 393224 | tf_op jit(solution)/shard_map/ppermute | solution.py:328
  121.5 30.7 %collective-permute-start.21 = (f32[2,2,8,8,128]{4,3,2,1,0:T(8,128)S(1)}, f32[2,2,8,8,128]{4,3,2,1,0:T(8,128)S(1)}, u32[]{:S(2)}, u32[]{:S(2)}) collective-permute-start(f32[2,2,8,8,128]{4,3,2,1,0:T(8,128)S(1)} %get-tuple-element.59), channel_id=1, source_target_pairs={{0,22},{1,23},{2,20},{3,21},{4,18},{5,19},{6,16},{7,17},{8,30},{9,... | collective-permute-start | bytes 393224 | tf_op jit(solution)/shard_map/ppermute | solution.py:328
  132.7 25.3 %collective-permute-start.22 = (f32[2,2,8,8,128]{4,3,2,1,0:T(8,128)S(1)}, f32[2,2,8,8,128]{4,3,2,1,0:T(8,128)S(1)}, u32[]{:S(2)}, u32[]{:S(2)}) collective-permute-start(f32[2,2,8,8,128]{4,3,2,1,0:T(8,128)S(1)} %get-tuple-element.60), channel_id=1, source_target_pairs={{0,23},{1,22},{2,21},{3,20},{4,19},{5,18},{6,17},{7,16},{8,31},{9,... | collective-permute-start | bytes 393224 | tf_op jit(solution)/shard_map/ppermute | solution.py:328
  137.1 27.8 %collective-permute-start.23 = (f32[2,2,8,8,128]{4,3,2,1,0:T(8,128)S(1)}, f32[2,2,8,8,128]{4,3,2,1,0:T(8,128)S(1)}, u32[]{:S(2)}, u32[]{:S(2)}) collective-permute-start(f32[2,2,8,8,128]{4,3,2,1,0:T(8,128)S(1)} %get-tuple-element.61), channel_id=1, source_target_pairs={{0,24},{1,25},{2,26},{3,27},{4,28},{5,29},{6,30},{7,31},{8,16},{9,... | collective-permute-start | bytes 393224 | tf_op jit(solution)/shard_map/ppermute | solution.py:328
  144.0 35.0 %collective-permute-start.24 = (f32[2,2,8,8,128]{4,3,2,1,0:T(8,128)S(1)}, f32[2,2,8,8,128]{4,3,2,1,0:T(8,128)S(1)}, u32[]{:S(2)}, u32[]{:S(2)}) collective-permute-start(f32[2,2,8,8,128]{4,3,2,1,0:T(8,128)S(1)} %get-tuple-element.62), channel_id=1, source_target_pairs={{0,25},{1,24},{2,27},{3,26},{4,29},{5,28},{6,31},{7,30},{8,17},{9,... | collective-permute-start | bytes 393224 | tf_op jit(solution)/shard_map/ppermute | solution.py:328
  146.8 35.8 %collective-permute-start.25 = (f32[2,2,8,8,128]{4,3,2,1,0:T(8,128)S(1)}, f32[2,2,8,8,128]{4,3,2,1,0:T(8,128)S(1)}, u32[]{:S(2)}, u32[]{:S(2)}) collective-permute-start(f32[2,2,8,8,128]{4,3,2,1,0:T(8,128)S(1)} %get-tuple-element.63), channel_id=1, source_target_pairs={{0,26},{1,27},{2,24},{3,25},{4,30},{5,31},{6,28},{7,29},{8,18},{9,... | collective-permute-start | bytes 393224 | tf_op jit(solution)/shard_map/ppermute | solution.py:328
  152.2 33.2 %collective-permute-start.26 = (f32[2,2,8,8,128]{4,3,2,1,0:T(8,128)S(1)}, f32[2,2,8,8,128]{4,3,2,1,0:T(8,128)S(1)}, u32[]{:S(2)}, u32[]{:S(2)}) collective-permute-start(f32[2,2,8,8,128]{4,3,2,1,0:T(8,128)S(1)} %get-tuple-element.64), channel_id=1, source_target_pairs={{0,27},{1,26},{2,25},{3,24},{4,31},{5,30},{6,29},{7,28},{8,19},{9,... | collective-permute-start | bytes 393224 | tf_op jit(solution)/shard_map/ppermute | solution.py:328
  158.0 29.5 %collective-permute-start.27 = (f32[2,2,8,8,128]{4,3,2,1,0:T(8,128)S(1)}, f32[2,2,8,8,128]{4,3,2,1,0:T(8,128)S(1)}, u32[]{:S(2)}, u32[]{:S(2)}) collective-permute-start(f32[2,2,8,8,128]{4,3,2,1,0:T(8,128)S(1)} %get-tuple-element.65), channel_id=1, source_target_pairs={{0,28},{1,29},{2,30},{3,31},{4,24},{5,25},{6,26},{7,27},{8,20},{9,... | collective-permute-start | bytes 393224 | tf_op jit(solution)/shard_map/ppermute | solution.py:328
  164.9 25.4 %collective-permute-start.28 = (f32[2,2,8,8,128]{4,3,2,1,0:T(8,128)S(1)}, f32[2,2,8,8,128]{4,3,2,1,0:T(8,128)S(1)}, u32[]{:S(2)}, u32[]{:S(2)}) collective-permute-start(f32[2,2,8,8,128]{4,3,2,1,0:T(8,128)S(1)} %get-tuple-element.66), channel_id=1, source_target_pairs={{0,29},{1,28},{2,31},{3,30},{4,25},{5,24},{6,27},{7,26},{8,21},{9,... | collective-permute-start | bytes 393224 | tf_op jit(solution)/shard_map/ppermute | solution.py:328
  179.0 15.2 %collective-permute-start.29 = (f32[2,2,8,8,128]{4,3,2,1,0:T(8,128)S(1)}, f32[2,2,8,8,128]{4,3,2,1,0:T(8,128)S(1)}, u32[]{:S(2)}, u32[]{:S(2)}) collective-permute-start(f32[2,2,8,8,128]{4,3,2,1,0:T(8,128)S(1)} %get-tuple-element.67), channel_id=1, source_target_pairs={{0,30},{1,31},{2,28},{3,29},{4,26},{5,27},{6,24},{7,25},{8,22},{9,... | collective-permute-start | bytes 393224 | tf_op jit(solution)/shard_map/ppermute | solution.py:328
  182.5 14.4 %collective-permute-start.30 = (f32[2,2,8,8,128]{4,3,2,1,0:T(8,128)S(1)}, f32[2,2,8,8,128]{4,3,2,1,0:T(8,128)S(1)}, u32[]{:S(2)}, u32[]{:S(2)}) collective-permute-start(f32[2,2,8,8,128]{4,3,2,1,0:T(8,128)S(1)} %get-tuple-element.68), channel_id=1, source_target_pairs={{0,31},{1,30},{2,29},{3,28},{4,27},{5,26},{6,25},{7,24},{8,23},{9,... | collective-permute-start | bytes 393224 | tf_op jit(solution)/shard_map/ppermute | solution.py:328
  (8 other events, 598.2 us)
